TPU v7x, 128 devices: a whole 4x4x4 slice. The times are simulated.
128 devices in a mesh: ctx: 16 (over x, z_lo, core), grp: 8 (over y, z_hi).
Axes of the slice: x: 4, y: 4, z: 4 (z_hi: 2, z_lo: 2; z = z_hi * 2 + z_lo), core: 2. Of those that a mesh axis runs over, the one named last changes fastest.
Arguments:
- queries: bfloat16 [8, 4096, 6144], P('grp', 'ctx'), may hold values from -48 to 48
- key_states: bfloat16 [8, 4096, 6144], P('grp', 'ctx'), may hold values from -6 to 6
- value_states: bfloat16 [8, 4096, 4096], P('grp', 'ctx'), may hold values from -6 to 6
- out_grad: bfloat16 [8, 4096, 4096], P('grp', 'ctx'), may hold values from -6 to 6
- lse_rest: float32 [8, 32, 4096], P('grp', None, 'ctx'), may hold values from 5 to 9
- out_dot: float32 [8, 32, 4096], P('grp', None, 'ctx'), may hold values from -16 to 16
- moe_acts: bfloat16 [8, 9, 7168, 256], P('grp', None, 'ctx'), may hold values from -6 to 6
- moe_grads: bfloat16 [8, 9, 256, 1024], P('grp', None, 'ctx'), may hold values from -0.375 to 0.375
- counts: int32 [8, 9], replicated, may hold values from 64 to 256, as said below
- replica_list: int32 [8, 7], replicated, may hold values from 0 to 1
Outputs:
- query_grad: bfloat16 [8, 4096, 6144], P('grp', 'ctx')
- key_grad: bfloat16 [8, 4096, 6144], P('grp', 'ctx')
- value_grad: bfloat16 [8, 4096, 4096], P('grp', 'ctx')
- expert_grad: float32 [8, 2, 7168, 1024], P('grp', None, 'ctx')
Inputs may be any that keep to these rules, and one draw needn't show every extreme that they name: `counts`: in every group one slot holds exactly 256 live rows; every other slot holds between 64 and 128. Replica slot r of group g holds expert replica_list[g, r] of the 2 experts owned by group (g + r + 1) mod 8.
All inputs are finite; a program needn't handle non-finite values.
Results may differ from a plain program's by a relative error of at most 0.0075.
Values may be sent and summed in bfloat16 or wider, within the bound.
A program may use at most 256 MiB of HBM per device.

v0:
```python
import math

import jax
import jax.numpy as jnp
from jax import lax
from jax.sharding import PartitionSpec as P

QK_DIM = 192
V_DIM = 128
HEADS = 32


def from_behind(x, axis, by):
    length = lax.axis_size(axis)
    pairs = [(i, i + by) for i in range(length) if 0 <= i + by < length]
    return lax.ppermute(x, axis, pairs)


def passed_along(x, axis, by):
    length = lax.axis_size(axis)
    return lax.ppermute(x, axis, [(i, (i + by) % length) for i in range(length)])


def window_mask(position, block_rows):
    query_pos = lax.iota(jnp.int32, block_rows)[:, None]
    key_pos = lax.iota(jnp.int32, 3 * block_rows)[None, :]
    behind = 2 - key_pos // block_rows
    present = position - behind >= 0
    causal = (behind > 0) | (key_pos - 2 * block_rows <= query_pos)
    return present & causal


def half_round(value_in):
    return value_in.astype(jnp.bfloat16).astype(jnp.float32)


def pair_grads(query_rows, key_rows, value_rows, grad_rows, rest_rows, dot_rows, allowed):
    score_scale = query_rows.shape[2] ** (-0.5)
    block_rows = query_rows.shape[0]
    scores = (
        jnp.einsum("qhd,khd->hqk", query_rows, key_rows, preferred_element_type=jnp.float32)
        * score_scale
    )
    masked = jnp.where(allowed[None], scores, -1e30)
    row_max = jnp.max(masked, axis=2, keepdims=True)
    window = row_max[:, :, 0] + jnp.log(jnp.sum(jnp.exp(masked - row_max), axis=2))
    combined = jnp.logaddexp(window, rest_rows)
    attn_prob = jnp.where(allowed[None], jnp.exp(masked - combined[:, :, None]), 0.0)
    prob_grad = jnp.einsum(
        "qhv,khv->hqk", grad_rows, value_rows, preferred_element_type=jnp.float32
    )
    dscore = (attn_prob * (prob_grad - dot_rows[:, :, None])).astype(jnp.bfloat16)
    prob_half = attn_prob.astype(jnp.bfloat16)

    def query_term(offset):
        return (
            jnp.einsum(
                "hqk,khd->qhd",
                dscore[:, :, offset : offset + block_rows],
                key_rows[offset : offset + block_rows],
                preferred_element_type=jnp.float32,
            )
            * score_scale
        )

    query_grad = (
        query_term(2 * block_rows) + half_round(query_term(block_rows)) + half_round(query_term(0))
    )
    key_grad = (
        jnp.einsum("hqk,qhd->khd", dscore, query_rows, preferred_element_type=jnp.float32)
        * score_scale
    )
    value_grad = jnp.einsum(
        "hqk,qhv->khv", prob_half, grad_rows, preferred_element_type=jnp.float32
    )
    return (query_grad, key_grad, value_grad)


def merge_heads(stacked):
    moved = jnp.moveaxis(stacked, 0, 1)
    return moved.reshape(moved.shape[0], moved.shape[1] * moved.shape[2] * moved.shape[3])


def window_grads(
    queries, key_states, value_states, out_grad, lse_rest, out_dot, near_blocks, far_blocks
):
    block_rows = queries.shape[1]
    position = lax.axis_index("ctx")
    key_rows = jnp.concatenate([far_blocks[0][0], near_blocks[0][0], key_states[0]], 0).reshape(
        3 * block_rows, HEADS, QK_DIM
    )
    value_rows = jnp.concatenate([far_blocks[1][0], near_blocks[1][0], value_states[0]], 0).reshape(
        3 * block_rows, HEADS, V_DIM
    )
    query_rows = queries[0].reshape(block_rows, HEADS, QK_DIM)
    grad_rows = out_grad[0].reshape(block_rows, HEADS, V_DIM)
    allowed = window_mask(position, block_rows)
    group_size = math.gcd(HEADS, 8)

    def head_block(head_group):
        head_start = head_group * group_size

        def head_slice(source_array, along):
            return lax.dynamic_slice_in_dim(source_array, head_start, group_size, along)

        return pair_grads(
            head_slice(query_rows, 1),
            head_slice(key_rows, 1),
            head_slice(value_rows, 1),
            head_slice(grad_rows, 1),
            head_slice(lse_rest[0], 0),
            head_slice(out_dot[0], 0),
            allowed,
        )

    query_parts, key_parts, value_parts = lax.map(
        head_block, lax.iota(jnp.int32, HEADS // group_size)
    )
    return (merge_heads(query_parts), merge_heads(key_parts), merge_heads(value_parts))


def attention_part(queries, key_states, value_states, out_grad, lse_rest, out_dot):
    block_rows = queries.shape[1]
    near_blocks = from_behind((key_states, value_states), "ctx", 1)
    far_blocks = from_behind((key_states, value_states), "ctx", 2)
    query_grad, key_grad, value_grad = window_grads(
        queries, key_states, value_states, out_grad, lse_rest, out_dot, near_blocks, far_blocks
    )
    returned_near = from_behind(
        (
            key_grad[block_rows : 2 * block_rows].astype(jnp.bfloat16),
            value_grad[block_rows : 2 * block_rows].astype(jnp.bfloat16),
        ),
        "ctx",
        -1,
    )
    returned_far = from_behind(
        (key_grad[:block_rows].astype(jnp.bfloat16), value_grad[:block_rows].astype(jnp.bfloat16)),
        "ctx",
        -2,
    )
    key_total = (
        key_grad[2 * block_rows :]
        + returned_near[0].astype(jnp.float32)
        + returned_far[0].astype(jnp.float32)
    )
    value_total = (
        value_grad[2 * block_rows :]
        + returned_near[1].astype(jnp.float32)
        + returned_far[1].astype(jnp.float32)
    )
    return (
        query_grad.astype(jnp.bfloat16)[None],
        key_total.astype(jnp.bfloat16)[None],
        value_total.astype(jnp.bfloat16)[None],
    )


def table_row(lookup, wanted):
    row_hits = (lax.iota(jnp.int32, lookup.shape[0]) == wanted)[:, None]
    return jnp.sum(jnp.where(row_hits, lookup, 0), axis=0)


def slot_partials(activations, hidden_grads, live_count):
    row_piece = lax.all_gather(hidden_grads, "ctx", axis=1, tiled=True)
    piece_rows = row_piece.shape[1]
    row_ids = lax.iota(jnp.int32, piece_rows)
    live_rows = row_ids[None, :] < live_count[:, None]
    masked = jnp.where(live_rows[:, :, None], row_piece, jnp.zeros_like(row_piece))
    return jnp.einsum("sdr,srf->sdf", activations, masked, preferred_element_type=jnp.float32)


def expert_part(moe_acts, moe_grads, counts, replica_list):
    activations = moe_acts[0]
    hidden_grads = moe_grads[0]
    group_index = lax.axis_index("grp")
    groups_total = lax.axis_size("grp")
    replicas = replica_list.shape[1]
    own_count = activations.shape[0] - replicas
    my_counts = table_row(counts, group_index)
    owned_ids = lax.iota(jnp.int32, own_count)
    partial_value = slot_partials(activations, hidden_grads, my_counts)
    summed = partial_value[:own_count]
    for replica in range(replicas):
        incoming = passed_along(partial_value[own_count + replica], "grp", replica + 1)
        source = (group_index - 1 - replica) % groups_total
        chosen = table_row(replica_list, source)[replica]
        weight = (owned_ids == chosen).astype(jnp.float32)
        summed = summed + weight[:, None, None] * incoming[None]
    return summed[None]


def local(
    queries,
    key_states,
    value_states,
    out_grad,
    lse_rest,
    out_dot,
    moe_acts,
    moe_grads,
    counts,
    replica_list,
):
    query_grad, key_grad, value_grad = attention_part(
        queries, key_states, value_states, out_grad, lse_rest, out_dot
    )
    expert_grad = expert_part(moe_acts, moe_grads, counts, replica_list)
    return (query_grad, key_grad, value_grad, expert_grad)


def solution(mesh):
    return jax.shard_map(
        local,
        mesh=mesh,
        in_specs=(
            P("grp", "ctx", None),
            P("grp", "ctx", None),
            P("grp", "ctx", None),
            P("grp", "ctx", None),
            P("grp", None, "ctx"),
            P("grp", None, "ctx"),
            P("grp", None, "ctx", None),
            P("grp", None, "ctx", None),
            P(),
            P(),
        ),
        out_specs=(
            P("grp", "ctx", None),
            P("grp", "ctx", None),
            P("grp", "ctx", None),
            P("grp", None, "ctx", None),
        ),
        check_vma=False,
    )
```

profile of v0, /device:TPU:26, one launch (start us, length us, event | category | flops | bytes accessed | tf_op | source)
XLA Modules:
  0.0 743.6 jit_solution(14842371811887629661)
XLA Ops:
  23.9 4.6 copy.29
  37.4 144.2 %collective-permute-done.3 = bf16[1,256,4096]{1,2,0:T(8,128)(2,1)} collective-permute-done((bf16[1,256,4096]{1,2,0:T(8,128)(2,1)}, bf16[1,256,4096]{1,2,0:T(8,128)(2,1)}, u32[]{:S(2)}, u32[]{:S(2)}) %collective-permute-start.3) | collective-permute-done | bytes 2097184 | tf_op jit(solution)/shard_map/ppermute | solution.py:16
  181.6 6.2 pad_maximum_fusion.1
  192.5 4.7 copy.27
  197.2 8.9 %pad_maximum_fusion = bf16[768,32,192]{0,2,1:T(8,128)(2,1)} fusion(bf16[256,32,192]{0,2,1:T(8,128)(2,1)} %bitcast.109, bf16[256,32,192]{0,2,1:T(8,128)(2,1)} %bitcast.110, bf16[256,32,192]{0,2,1:T(8,128)(2,1)} %bitcast.111), kind=kLoop, calls=%fused_computation.52 | loop fusion | flops 28311552 | bytes 18874368 | tf_op jit(solution)/shard_map/concatenate | solution.py:89
  206.1 120.9 %while.15 = (s32[]{:T(128)}, bf16[4,256,8,192]{1,3,2,0:T(8,128)(2,1)}, f32[4,768,8,192]{1,3,2,0:T(8,128)}, f32[4,768,8,128]{1,3,2,0:T(8,128)}, s32[4]{0:T(128)S(...) while((s32[]{:T(128)}, ...), condition=%wide.region_3.4_spmd.clone, body=%wide.region_0.3_spmd.clone.sunk | while | flops 2652452864 | bytes 115383208 | solution.py:116
  214.3 6.0 multiply_convert_fusion.5
  231.7 4.7 bitcast_dynamic-update-slice_fusion.8
  244.5 6.0 multiply_convert_fusion.5
  274.7 6.0 multiply_convert_fusion.5
  305.0 6.0 multiply_convert_fusion.5
  322.4 4.7 bitcast_dynamic-update-slice_fusion.8
  327.0 8.1 %bitcast_convert_fusion = bf16[768,4,8,128]{0,3,2,1:T(8,128)(2,1)} fusion(f32[4,768,8,128]{1,3,2,0:T(8,128)} %get-tuple-element.70), kind=kLoop, calls=%fused_computation.115 | loop fusion | flops 3145728 | bytes 18874368 | tf_op jit(solution)/shard_map/convert.2
  335.1 4.7 fusion.63
  346.9 7.0 bitcast_convert_fusion.1
  359.3 23.8 %collective-permute-start.4 = (bf16[256,6144]{0,1:T(8,128)(2,1)}, bf16[256,6144]{0,1:T(8,128)(2,1)}, u32[]{:S(2)}, u32[]{:S(2)}) collective-permute-start(bf16[256,6144]{0,1:T(8,128)(2,1)} %bitcast.12), channel_id=1, source_target_pairs={{8,0},{16,8},{24,16},{32,24},{40,32},{48,40},{56,48},{64,56},{72,6... | collective-permute-start | bytes 9437192 | tf_op jit(solution)/shard_map/ppermute | solution.py:16
  389.2 10.4 %convolution_bitcast_fusion = f32[9,448,1024]{2,1,0:T(8,128)} fusion(bf16[1,9,256,1024]{3,2,1,0:T(8,128)(2,1)} %all-gather.3.cloned.1.call-done, pred[9,256]{1,0:T(8,128)(4,1)S(1)} %iota_compare_fusion.1, bf16[1,9,448,256]{3,2,1,0:T(8,128)(2,1)S(1)} %copy-done), kind=kOutput, calls=%fused_computation.53 | convolution fusion | flops 2116288512 | bytes 23300352 | tf_op jit(solution)/shard_map/sdr,srf->sdf/dot_general | solution.py:170
  399.6 9.7 %slice_bitcast_fusion.6 = (f32[448,1024]{1,0:T(8,128)}, f32[448,1024]{1,0:T(8,128)}, f32[448,1024]{1,0:T(8,128)}, f32[448,1024]{1,0:T(8,128)}, f32[448,1024]{1,0...) fusion(f32[9,448,1024]{2,1,0:T(8,128)} %convolution_bitcast_fusion), kind=kLoop, calls=%fused_computation.78 | loop fusion | bytes 25690112 | tf_op jit(solution)/shard_map/squeeze | solution.py:185
  421.1 4.6 copy.40
  425.8 6.1 slice.127
  436.4 5.6 copy.43
  442.0 180.2 %collective-permute-done.6 = bf16[256,4096]{1,0:T(8,128)(2,1)} collective-permute-done((bf16[256,4096]{1,0:T(8,128)(2,1)}, bf16[256,4096]{1,0:T(8,128)(2,1)}, u32[]{:S(2)}, u32[]{:S(2)}) %collective-permute-start.6) | collective-permute-done | bytes 2097184 | tf_op jit(solution)/shard_map/ppermute | solution.py:16
  622.2 5.7 collective-permute-start.10
  627.9 11.2 %collective-permute-start.9 = (f32[448,1024]{1,0:T(8,128)}, f32[448,1024]{1,0:T(8,128)}, u32[]{:S(2)}, u32[]{:S(2)}) collective-permute-start(f32[448,1024]{1,0:T(8,128)} %get-tuple-element.165), channel_id=1, source_target_pairs={{0,2},{1,3},{2,4},{3,5},{4,6},{5,7},{6,0},{7,1},{8,10},{9,11},{10,... | collective-permute-start | bytes 5505032 | tf_op jit(solution)/shard_map/ppermute | solution.py:21
  639.1 5.8 fusion.52
  644.9 7.2 fusion.42
  652.1 4.6 copy.41
  656.7 5.9 collective-permute-done.12
  662.9 38.8 %collective-permute-done.10 = f32[448,1024]{1,0:T(8,128)} collective-permute-done((f32[448,1024]{1,0:T(8,128)}, f32[448,1024]{1,0:T(8,128)}, u32[]{:S(2)}, u32[]{:S(2)}) %collective-permute-start.10) | collective-permute-done | bytes 1835040 | tf_op jit(solution)/shard_map/ppermute | solution.py:21
  701.8 15.3 %collective-permute-done.9 = f32[448,1024]{1,0:T(8,128)} collective-permute-done((f32[448,1024]{1,0:T(8,128)}, f32[448,1024]{1,0:T(8,128)}, u32[]{:S(2)}, u32[]{:S(2)}) %collective-permute-start.9) | collective-permute-done | bytes 1835040 | tf_op jit(solution)/shard_map/ppermute | solution.py:21
  717.1 11.2 %collective-permute-done.8 = f32[448,1024]{1,0:T(8,128)} collective-permute-done((f32[448,1024]{1,0:T(8,128)}, f32[448,1024]{1,0:T(8,128)}, u32[]{:S(2)}, u32[]{:S(2)}) %collective-permute-start.8) | collective-permute-done | bytes 1835040 | tf_op jit(solution)/shard_map/ppermute | solution.py:21
  728.3 8.4 %fusion.50 = f32[1,2,448,1024]{3,2,1,0:T(8,128)} fusion(f32[9,448,1024]{2,1,0:T(8,128)} %convolution_bitcast_fusion, f32[448,1024]{1,0:T(8,128)} %collective-permute-done.14, f32[2]{0:T(128)S(1)} %compare_convert_fusion, f32[448,1024]{1,0:T(8,128)} %collective-permute-done.13, f32[2]{0:T(128)S(1)} %compare_convert_fusion.1, ...), kind=kLoop, calls=%fused_computation.68 | loop fusion | flops 12845056 | bytes 20185144 | tf_op jit(solution)/shard_map/broadcast_in_dim | solution.py:190
  (143 shorter events, 150.1 us)
Async XLA Ops:
  7.2 382.0 %copy-start = (bf16[1,9,448,256]{3,2,1,0:T(8,128)(2,1)S(1)}, bf16[1,9,448,256]{3,2,1,0:T(8,128)(2,1)}, u32[]{:S(2)}) copy-start(bf16[1,9,448,256]{3,2,1,0:T(8,128)(2,1)} %param.18) | copy-start | bytes 6193156
  7.2 382.0 %all-gather.3.cloned.1.call-start = ((), (), s32[]{:S(2)}) async-start(), calls=%async_computation | async-start | bytes 5013504 | tf_op jit(solution)/shard_map/all_gather | solution.py:165
  7.2 180.6 %collective-permute-start.1 = (bf16[1,256,6144]{2,1,0:T(8,128)(2,1)}, bf16[1,256,6144]{2,1,0:T(8,128)(2,1)}, u32[]{:S(2)}, u32[]{:S(2)}) collective-permute-start(bf16[1,256,6144]{2,1,0:T(8,128)(2,1)} %param.13), channel_id=1, source_target_pairs={{0,8},{8,16},{16,24},{24,32},{32,40},{40,48},{48,56},{56,64},{64,7... | collective-permute-start | bytes 9437192 | tf_op jit(solution)/shard_map/ppermute | solution.py:16
  9.3 183.2 %collective-permute-start = (bf16[1,256,6144]{2,1,0:T(8,128)(2,1)}, bf16[1,256,6144]{2,1,0:T(8,128)(2,1)}, u32[]{:S(2)}, u32[]{:S(2)}) collective-permute-start(bf16[1,256,6144]{2,1,0:T(8,128)(2,1)} %param.13), channel_id=1, source_target_pairs={{0,16},{8,24},{16,32},{24,40},{32,48},{40,56},{48,64},{56,72},{64,... | collective-permute-start | bytes 9437192 | tf_op jit(solution)/shard_map/ppermute | solution.py:16
  17.2 164.4 %collective-permute-start.3 = (bf16[1,256,4096]{1,2,0:T(8,128)(2,1)}, bf16[1,256,4096]{1,2,0:T(8,128)(2,1)}, u32[]{:S(2)}, u32[]{:S(2)}) collective-permute-start(bf16[1,256,4096]{1,2,0:T(8,128)(2,1)} %copy.32), channel_id=1, source_target_pairs={{0,8},{8,16},{16,24},{24,32},{32,40},{40,48},{48,56},{56,64},{64,7... | collective-permute-start | bytes 6291464 | tf_op jit(solution)/shard_map/ppermute | solution.py:16
  20.0 161.7 %collective-permute-start.2 = (bf16[1,256,4096]{1,2,0:T(8,128)(2,1)}, bf16[1,256,4096]{1,2,0:T(8,128)(2,1)}, u32[]{:S(2)}, u32[]{:S(2)}) collective-permute-start(bf16[1,256,4096]{1,2,0:T(8,128)(2,1)} %copy.32), channel_id=1, source_target_pairs={{0,16},{8,24},{16,32},{24,40},{32,48},{40,56},{48,64},{56,72},{64,... | collective-permute-start | bytes 6291464 | tf_op jit(solution)/shard_map/ppermute | solution.py:16
  33.1 4.1 copy-start.3
  211.1 3.1 copy-start.1
  224.7 7.0 slice-start
  227.5 4.2 slice-start.1
  241.4 3.1 copy-start.1
  255.0 7.0 slice-start
  257.7 4.3 slice-start.1
  271.5 3.1 copy-start.1
  282.7 2.5 copy-start.2
  285.1 7.1 slice-start
  287.9 4.3 slice-start.1
  301.8 3.1 copy-start.1
  315.4 7.0 slice-start
  318.1 4.2 slice-start.1
  344.0 69.1 %collective-permute-start.7 = (bf16[256,4096]{1,0:T(8,128)(2,1)}, bf16[256,4096]{1,0:T(8,128)(2,1)}, u32[]{:S(2)}, u32[]{:S(2)}) collective-permute-start(bf16[256,4096]{1,0:T(8,128)(2,1)} %copy.45), channel_id=1, source_target_pairs={{16,0},{24,8},{32,16},{40,24},{48,32},{56,40},{64,48},{72,56},{80,... | collective-permute-start | bytes 6291464 | tf_op jit(solution)/shard_map/ppermute | solution.py:16
  357.4 264.9 %collective-permute-start.5 = (bf16[256,6144]{0,1:T(8,128)(2,1)}, bf16[256,6144]{0,1:T(8,128)(2,1)}, u32[]{:S(2)}, u32[]{:S(2)}) collective-permute-start(bf16[256,6144]{0,1:T(8,128)(2,1)} %bitcast.13), channel_id=1, source_target_pairs={{16,0},{24,8},{32,16},{40,24},{48,32},{56,40},{64,48},{72,56},{80,... | collective-permute-start | bytes 9437192 | tf_op jit(solution)/shard_map/ppermute | solution.py:16
  359.3 263.0 %collective-permute-start.4 = (bf16[256,6144]{0,1:T(8,128)(2,1)}, bf16[256,6144]{0,1:T(8,128)(2,1)}, u32[]{:S(2)}, u32[]{:S(2)}) collective-permute-start(bf16[256,6144]{0,1:T(8,128)(2,1)} %bitcast.12), channel_id=1, source_target_pairs={{8,0},{16,8},{24,16},{32,24},{40,32},{48,40},{56,48},{64,56},{72,6... | collective-permute-start | bytes 9437192 | tf_op jit(solution)/shard_map/ppermute | solution.py:16
  387.2 235.0 %collective-permute-start.6 = (bf16[256,4096]{1,0:T(8,128)(2,1)}, bf16[256,4096]{1,0:T(8,128)(2,1)}, u32[]{:S(2)}, u32[]{:S(2)}) collective-permute-start(bf16[256,4096]{1,0:T(8,128)(2,1)} %copy.44), channel_id=1, source_target_pairs={{8,0},{16,8},{24,16},{32,24},{40,32},{48,40},{56,48},{64,56},{72,6... | collective-permute-start | bytes 6291464 | tf_op jit(solution)/shard_map/ppermute | solution.py:16
  399.6 14.0 %copy-start.4 = (s32[8,7]{1,0:T(8,128)S(1)}, s32[8,7]{1,0:T(8,128)}, u32[]{:S(2)}) copy-start(s32[8,7]{1,0:T(8,128)} %param.21) | copy-start | bytes 676
  409.3 218.7 %collective-permute-start.14 = (f32[448,1024]{1,0:T(8,128)}, f32[448,1024]{1,0:T(8,128)}, u32[]{:S(2)}, u32[]{:S(2)}) collective-permute-start(f32[448,1024]{1,0:T(8,128)} %get-tuple-element.160), channel_id=1, source_target_pairs={{0,7},{1,0},{2,1},{3,2},{4,3},{5,4},{6,5},{7,6},{8,15},{9,8},{10,9... | collective-permute-start | bytes 5505032 | tf_op jit(solution)/shard_map/ppermute | solution.py:21
  413.0 226.1 %collective-permute-start.13 = (f32[448,1024]{1,0:T(8,128)}, f32[448,1024]{1,0:T(8,128)}, u32[]{:S(2)}, u32[]{:S(2)}) collective-permute-start(f32[448,1024]{1,0:T(8,128)} %get-tuple-element.161), channel_id=1, source_target_pairs={{0,6},{1,7},{2,0},{3,1},{4,2},{5,3},{6,4},{7,5},{8,14},{9,15},{10,... | collective-permute-start | bytes 5505032 | tf_op jit(solution)/shard_map/ppermute | solution.py:21
  622.2 40.4 %collective-permute-start.12 = (f32[448,1024]{1,0:T(8,128)}, f32[448,1024]{1,0:T(8,128)}, u32[]{:S(2)}, u32[]{:S(2)}) collective-permute-start(f32[448,1024]{1,0:T(8,128)} %get-tuple-element.162), channel_id=1, source_target_pairs={{0,5},{1,6},{2,7},{3,0},{4,1},{5,2},{6,3},{7,4},{8,13},{9,14},{10,... | collective-permute-start | bytes 5505032 | tf_op jit(solution)/shard_map/ppermute | solution.py:21
  622.2 40.7 %collective-permute-start.11 = (f32[448,1024]{1,0:T(8,128)}, f32[448,1024]{1,0:T(8,128)}, u32[]{:S(2)}, u32[]{:S(2)}) collective-permute-start(f32[448,1024]{1,0:T(8,128)} %get-tuple-element.163), channel_id=1, source_target_pairs={{0,4},{1,5},{2,6},{3,7},{4,0},{5,1},{6,2},{7,3},{8,12},{9,13},{10,... | collective-permute-start | bytes 5505032 | tf_op jit(solution)/shard_map/ppermute | solution.py:21
  622.2 79.6 %collective-permute-start.10 = (f32[448,1024]{1,0:T(8,128)}, f32[448,1024]{1,0:T(8,128)}, u32[]{:S(2)}, u32[]{:S(2)}) collective-permute-start(f32[448,1024]{1,0:T(8,128)} %get-tuple-element.164), channel_id=1, source_target_pairs={{0,3},{1,4},{2,5},{3,6},{4,7},{5,0},{6,1},{7,2},{8,11},{9,12},{10,... | collective-permute-start | bytes 5505032 | tf_op jit(solution)/shard_map/ppermute | solution.py:21
  627.9 89.1 %collective-permute-start.9 = (f32[448,1024]{1,0:T(8,128)}, f32[448,1024]{1,0:T(8,128)}, u32[]{:S(2)}, u32[]{:S(2)}) collective-permute-start(f32[448,1024]{1,0:T(8,128)} %get-tuple-element.165), channel_id=1, source_target_pairs={{0,2},{1,3},{2,4},{3,5},{4,6},{5,7},{6,0},{7,1},{8,10},{9,11},{10,... | collective-permute-start | bytes 5505032 | tf_op jit(solution)/shard_map/ppermute | solution.py:21
  639.1 89.2 %collective-permute-start.8 = (f32[448,1024]{1,0:T(8,128)}, f32[448,1024]{1,0:T(8,128)}, u32[]{:S(2)}, u32[]{:S(2)}) collective-permute-start(f32[448,1024]{1,0:T(8,128)} %get-tuple-element.159), channel_id=1, source_target_pairs={{0,1},{1,2},{2,3},{3,4},{4,5},{5,6},{6,7},{7,0},{8,9},{9,10},{10,1... | collective-permute-start | bytes 5505032 | tf_op jit(solution)/shard_map/ppermute | solution.py:21
  (3 other events, 7.4 us)
Sparse Core Ops, SparseCore 0:
  23.9 53.2 all-gather.2
where the time goes:
time: 746 us; the launch traced here: 744 us
  waiting for transfers between devices  396 us (53%)
  matrix products  112 us (15%)
  local copies, waits for them, and re-layouts  88.8 us (12%)
  other arithmetic  65.9 us (9%)
  starting transfers between devices  64.1 us (9%)
  between operations  14.3 us (2%)
    ppermute x8, waiting for transfers between devices, from_behind(): return lax.ppermute(x, axis, pairs)  324 us
    ppermute x7, waiting for transfers between devices, passed_along(): lax.ppermute(x, axis, [(i, (i + by) % length) for i in range(length)])  71.6 us
    ppermute x8, starting transfers between devices, from_behind(): return lax.ppermute(x, axis, pairs)  43 us
    dot_general x12, matrix products, query_term(): jnp.einsum('hqk,khd->qhd', dscore[:, :, offset:offset + block_rows], key_...  27.3 us
    unnamed x12, local copies, waits for them, and re-layouts  26.7 us
    dot_general x4, matrix products, pair_grads(): jnp.einsum('qhv,khv->hqk', grad_rows, value_rows, preferred_element_type=...  24 us
    ppermute x7, starting transfers between devices, passed_along(): lax.ppermute(x, axis, [(i, (i + by) % length) for i in range(length)])  21.1 us
    dot_general x4, matrix products, pair_grads(): jnp.einsum('hqk,qhv->khv', prob_half, grad_rows, preferred_element_type=j...  18.5 us
  transfers between devices with their start and end apart: 16, of which 7 were waited for; matrix products, arithmetic and copies ran while one was open for 34% of the time, Pallas kernels for 0%

commit v1 on v0

v1 whole, which is shorter than its diff:
```python
import functools

import jax
import jax.numpy as jnp
from jax import lax
from jax.experimental import pallas as pl
from jax.experimental.pallas import tpu as pltpu
from jax.sharding import PartitionSpec as P

QK_DIM = 192
V_DIM = 128
PAIR_QK = 2 * QK_DIM
PAIR_V = 2 * V_DIM
AHEAD = 3
SCALE = QK_DIM**-0.5
LOW = -1e38
MESH = pl.DeviceIdType.MESH

M_Q, M_G, M_K, M_V, M_DQ, M_MS, M_W, M_DK, M_DV, M_DOT = range(10)


def rows_by_rows(a, b):
    return lax.dot_general(a, b, (((1,), (1,)), ((), ())), preferred_element_type=jnp.float32)


def plain(a, b):
    return lax.dot_general(a, b, (((1,), (0,)), ((), ())), preferred_element_type=jnp.float32)


def columns_by_rows(a, b):
    return lax.dot_general(a, b, (((0,), (0,)), ((), ())), preferred_element_type=jnp.float32)


def heads_of(ref, start, low_lanes, high_lanes):
    first = ref[:, pl.ds(start, 128)]
    middle = ref[:, pl.ds(pl.multiple_of(start + 128, 128), 128)]
    last = ref[:, pl.ds(pl.multiple_of(start + 256, 128), 128)]
    return (
        jnp.concatenate([first, middle * low_lanes], 1),
        jnp.concatenate([middle * high_lanes, last], 1),
    )


def store_pair(ref, index, even, odd):
    start = index
    kind = ref.dtype
    ref[:, pl.ds(start, 128)] = even[:, :128].astype(kind)
    ref[:, pl.ds(pl.multiple_of(start + 128, 128), 128)] = (even[:, 128:] + odd[:, :128]).astype(kind)
    ref[:, pl.ds(pl.multiple_of(start + 256, 128), 128)] = odd[:, 128:].astype(kind)


def attention_kernel(
    pairs,
    q,
    k,
    v,
    g,
    rest,
    dot,
    dq,
    dk,
    dv,
    qn,
    gn,
    dotn,
    ko,
    vo,
    dqs,
    dks,
    dvs,
    mss,
    msr,
    own_ms,
    ws,
    wr,
    fo,
    pring,
    dring,
    acck,
    accv,
    q2,
    g2,
    send,
    recv,
):
    rows = q.shape[0]
    me = lax.axis_index("ctx")
    total = lax.axis_size("ctx")
    core = lax.rem(me, 2)
    ahead_chip = lax.rem(me + 2, total)
    behind_chip = lax.rem(me + total - 2, total)
    other = me + 1 - 2 * core
    core_zero = core == 0
    c0 = jnp.where(core_zero, 1.0, 0.0).astype(jnp.float32)
    c1 = 1.0 - c0
    has_behind = me >= 2

    def qk_cols(pair):
        return pl.ds(pl.multiple_of(pair * PAIR_QK, 128), PAIR_QK)

    def v_cols(pair):
        return pl.ds(pl.multiple_of(pair * PAIR_V, 128), PAIR_V)

    def message(kind, pair):
        src, dst, target = {
            M_Q: lambda: (q.at[:, qk_cols(pair)], qn.at[:, qk_cols(pair)], behind_chip),
            M_G: lambda: (g.at[:, v_cols(pair)], gn.at[:, v_cols(pair)], behind_chip),
            M_K: lambda: (k.at[:, qk_cols(pair)], ko.at[:, qk_cols(pair)], other),
            M_V: lambda: (v.at[:, v_cols(pair)], vo.at[:, v_cols(pair)], other),
            M_DQ: lambda: (dqs.at[:, qk_cols(pair)], dq.at[:, qk_cols(pair)], ahead_chip),
            M_MS: lambda: (mss.at[pair], msr.at[pair], ahead_chip),
            M_W: lambda: (ws.at[pair], wr.at[pair], behind_chip),
            M_DK: lambda: (dks.at[:, qk_cols(pair)], dk.at[:, qk_cols(pair)], other),
            M_DV: lambda: (dvs.at[:, v_cols(pair)], dv.at[:, v_cols(pair)], other),
            M_DOT: lambda: (dot, dotn, behind_chip),
        }[kind]()
        return pltpu.make_async_remote_copy(
            src_ref=src,
            dst_ref=dst,
            send_sem=send.at[kind, pair],
            recv_sem=recv.at[kind, pair],
            device_id={"ctx": target},
            device_id_type=MESH,
        )

    barrier = pltpu.get_barrier_semaphore()
    for partner in (behind_chip, ahead_chip, other):
        pl.semaphore_signal(barrier, inc=1, device_id={"ctx": partner}, device_id_type=MESH)
    pl.semaphore_wait(barrier, 3)

    message(M_DOT, 0).start()
    for pair in range(min(AHEAD, pairs)):
        for kind in (M_Q, M_G, M_K, M_V):
            message(kind, pair).start()

    lane = lax.broadcasted_iota(jnp.int32, (1, 128), 1)
    low_lanes = jnp.where(lane < 64, 1.0, 0.0).astype(jnp.bfloat16)
    high_lanes = jnp.where(lane < 64, 0.0, 1.0).astype(jnp.bfloat16)
    is_low = lane < 64

    def pick_second(pair):
        @pl.when(core_zero)
        def _():
            q2[...] = qn[:, qk_cols(pair)]
            g2[...] = gn[:, v_cols(pair)]

        @pl.when(jnp.logical_not(core_zero))
        def _():
            q2[...] = q[:, qk_cols(pair)]
            g2[...] = g[:, v_cols(pair)]

    def v_head(ref, pair, head):
        return ref[:, pl.ds(pl.multiple_of(pair * PAIR_V + head * V_DIM, 128), V_DIM)]

    def first_phase(pair):
        for kind in (M_Q, M_G, M_K, M_V):
            message(kind, pair).wait_recv()

        @pl.when(pair == 0)
        def _():
            message(M_DOT, 0).wait_recv()

        @pl.when(pair + AHEAD < pairs)
        def _():
            for kind in (M_Q, M_G, M_K, M_V):
                message(kind, pair + AHEAD).start()

        pick_second(pair)
        slot = lax.rem(pair, 3)
        start = pl.multiple_of(pair * PAIR_QK, 128)
        k_own = heads_of(k, start, low_lanes, high_lanes)
        k_oth = heads_of(ko, start, low_lanes, high_lanes)
        q_own = heads_of(q, start, low_lanes, high_lanes)
        q_new = heads_of(qn, start, low_lanes, high_lanes)
        q_sec = heads_of(q2, 0, low_lanes, high_lanes)
        key_pos = lax.broadcasted_iota(jnp.int32, (rows, rows), 0)
        query_pos = lax.broadcasted_iota(jnp.int32, (rows, rows), 1)
        allowed = key_pos <= query_pos
        dot_new = dotn[pair]
        dot_own = dot[pair]
        dot_sec = c0 * dot_new + c1 * dot_own
        tops, sums, tops_own, sums_own, dq_heads = [], [], [], [], []
        for head in range(2):
            s1 = rows_by_rows(k_own[head], q_new[head]) * SCALE
            s2 = rows_by_rows(k_oth[head], q_sec[head]) * SCALE
            s3 = rows_by_rows(k_own[head], q_own[head]) * SCALE
            s3 = jnp.where(allowed, s3, -1e30)
            m1 = jnp.max(s1, 0, keepdims=True)
            m2 = jnp.max(s2, 0, keepdims=True)
            m3 = jnp.max(s3, 0, keepdims=True)
            top_new = jnp.maximum(m1, jnp.where(core_zero, m2, LOW))
            top_own = jnp.maximum(m3, jnp.where(core_zero, LOW, m2))
            top_sec = jnp.where(core_zero, top_new, top_own)
            p1 = jnp.exp(s1 - top_new)
            p2 = jnp.exp(s2 - top_sec)
            p3 = jnp.exp(s3 - top_own)
            z1 = jnp.sum(p1, 0, keepdims=True)
            z2 = jnp.sum(p2, 0, keepdims=True)
            z3 = jnp.sum(p3, 0, keepdims=True)
            tops.append(top_new)
            sums.append(z1 + c0 * z2)
            tops_own.append(top_own)
            sums_own.append(z3 + c1 * z2)
            g1 = rows_by_rows(v_head(v, pair, head), v_head(gn, pair, head))
            g2_ = rows_by_rows(v_head(vo, pair, head), g2[:, head * V_DIM : (head + 1) * V_DIM])
            g3 = rows_by_rows(v_head(v, pair, head), v_head(g, pair, head))
            d1 = (p1 * (g1 - dot_new[head : head + 1])).astype(jnp.bfloat16)
            d2 = (p2 * (g2_ - dot_sec[head : head + 1])).astype(jnp.bfloat16)
            d3 = (p3 * (g3 - dot_own[head : head + 1])).astype(jnp.bfloat16)
            for task, (p_, d_) in enumerate(((p1, d1), (p2, d2), (p3, d3))):
                pring[slot, head * 3 + task] = p_.astype(jnp.bfloat16)
                dring[slot, head * 3 + task] = d_
            dq_heads.append(columns_by_rows(d1, k_own[head]) + c0 * columns_by_rows(d2, k_oth[head]))
        zero = jnp.zeros((4, rows), jnp.float32)
        mss[pair] = jnp.concatenate(tops + sums + [zero], 0)
        own_ms[pair] = jnp.concatenate(tops_own + sums_own + [zero], 0)
        message(M_MS, pair).start()
        store_pair(dqs, start, *dq_heads)
        message(M_DQ, pair).start()

    def second_phase(pair):
        message(M_MS, pair).wait_recv()
        theirs = msr[pair]
        ours = own_ms[pair]
        away = rest[pair]
        top_far = jnp.where(has_behind, theirs[0:2], LOW)
        top = jnp.maximum(jnp.maximum(ours[0:2], away), top_far)
        whole = (
            ours[2:4] * jnp.exp(ours[0:2] - top)
            + jnp.exp(away - top)
            + theirs[2:4] * jnp.exp(top_far - top)
        )
        total_lse = top + jnp.log(whole)
        zero = jnp.zeros((6, rows), jnp.float32)
        ws[pair] = jnp.concatenate([jnp.exp(top_far - total_lse), zero], 0)
        fo[pair] = jnp.concatenate([jnp.exp(ours[0:2] - total_lse), zero], 0)
        message(M_W, pair).start()

    def third_phase(pair):
        message(M_W, pair).wait_recv()
        message(M_DQ, pair).wait_recv()
        pick_second(pair)
        slot = lax.rem(pair, 3)
        start = pl.multiple_of(pair * PAIR_QK, 128)
        k_own = heads_of(k, start, low_lanes, high_lanes)
        k_oth = heads_of(ko, start, low_lanes, high_lanes)
        q_own = heads_of(q, start, low_lanes, high_lanes)
        q_new = heads_of(qn, start, low_lanes, high_lanes)
        q_sec = heads_of(q2, 0, low_lanes, high_lanes)
        new_weight = wr[pair]
        own_weight = fo[pair]
        far_weight = ws[pair]
        sec_weight = c0 * new_weight + c1 * own_weight
        eye = lax.broadcasted_iota(jnp.int32, (rows, rows), 0) == lax.broadcasted_iota(
            jnp.int32, (rows, rows), 1
        )
        dq_heads, dk_heads, dko_heads, columns = [], [], [], []
        acc = lax.rem(pair, 2)
        for head in range(2):
            weights = [w[head : head + 1] for w in (new_weight, sec_weight, own_weight)]
            probs = [
                (pring[slot, head * 3 + t].astype(jnp.float32) * weights[t]).astype(jnp.bfloat16)
                for t in range(3)
            ]
            grads = [
                (dring[slot, head * 3 + t].astype(jnp.float32) * (weights[t] * SCALE)).astype(
                    jnp.bfloat16
                )
                for t in range(3)
            ]
            accv[acc, :, head * V_DIM : (head + 1) * V_DIM] = plain(
                probs[0], v_head(gn, pair, head)
            ) + plain(probs[2], v_head(g, pair, head))
            dvs[:, pl.ds(pl.multiple_of(pair * PAIR_V + head * V_DIM, 128), V_DIM)] = plain(
                probs[1], g2[:, head * V_DIM : (head + 1) * V_DIM]
            ).astype(jnp.bfloat16)
            dk_heads.append(plain(grads[0], q_new[head]) + plain(grads[2], q_own[head]))
            dko_heads.append(plain(grads[1], q_sec[head]))
            dq_heads.append(
                columns_by_rows(grads[2], k_own[head])
                + c1 * columns_by_rows(grads[1], k_oth[head])
            )
            columns.append(
                jnp.sum(jnp.where(eye, far_weight[head : head + 1] * SCALE, 0.0), 1, keepdims=True)
            )
        store_pair(dks, start, *dko_heads)
        message(M_DV, pair).start()
        message(M_DK, pair).start()
        store_pair(acck.at[acc], 0, *dk_heads)
        first = pl.ds(start, 128)
        middle = pl.ds(pl.multiple_of(start + 128, 128), 128)
        last = pl.ds(pl.multiple_of(start + 256, 128), 128)
        even, odd = dq_heads
        dq[:, first] = (even[:, :128] + columns[0] * dq[:, first].astype(jnp.float32)).astype(dq.dtype)
        dq[:, middle] = (
            even[:, 128:]
            + odd[:, :128]
            + jnp.where(is_low, columns[0], columns[1]) * dq[:, middle].astype(jnp.float32)
        ).astype(dq.dtype)
        dq[:, last] = (odd[:, 128:] + columns[1] * dq[:, last].astype(jnp.float32)).astype(dq.dtype)

    def fourth_phase(pair):
        message(M_DK, pair).wait_recv()
        message(M_DV, pair).wait_recv()
        acc = lax.rem(pair, 2)
        dk[:, qk_cols(pair)] = (acck[acc] + dk[:, qk_cols(pair)].astype(jnp.float32)).astype(dk.dtype)
        dv[:, v_cols(pair)] = (accv[acc] + dv[:, v_cols(pair)].astype(jnp.float32)).astype(dv.dtype)

    def step(at, carry):
        for lag, phase in enumerate((first_phase, second_phase, third_phase, fourth_phase)):
            @pl.when((at >= lag) & (at < pairs + lag))
            def _(lag=lag, phase=phase):
                phase(at - lag)

        return carry

    lax.fori_loop(0, pairs + 3, step, 0)

    message(M_DOT, 0).wait_send()

    def drain(pair, carry):
        for kind in (M_Q, M_G, M_K, M_V, M_DQ, M_MS, M_W, M_DK, M_DV):
            message(kind, pair).wait_send()
        return carry

    lax.fori_loop(0, pairs, drain, 0)


def attention_part(queries, key_states, value_states, out_grad, lse_rest, out_dot):
    rows, qk = queries.shape[1:]
    vv = value_states.shape[2]
    pairs = qk // PAIR_QK
    half = jnp.bfloat16
    vmem = pl.BlockSpec(memory_space=pltpu.VMEM)
    small = pltpu.VMEM((pairs, 8, rows), jnp.float32)
    wide = pltpu.VMEM((rows, qk), half)
    narrow = pltpu.VMEM((rows, vv), half)
    outs = pl.pallas_call(
        functools.partial(attention_kernel, pairs),
        out_shape=[
            jax.ShapeDtypeStruct((rows, qk), half),
            jax.ShapeDtypeStruct((rows, qk), half),
            jax.ShapeDtypeStruct((rows, vv), half),
        ],
        in_specs=[vmem] * 6,
        out_specs=[vmem] * 3,
        scratch_shapes=[
            wide,
            narrow,
            pltpu.VMEM((pairs, 2, rows), jnp.float32),
            wide,
            narrow,
            wide,
            wide,
            narrow,
            small,
            small,
            small,
            small,
            small,
            small,
            pltpu.VMEM((3, 6, rows, rows), half),
            pltpu.VMEM((3, 6, rows, rows), half),
            pltpu.VMEM((2, rows, PAIR_QK), jnp.float32),
            pltpu.VMEM((2, rows, PAIR_V), jnp.float32),
            pltpu.VMEM((rows, PAIR_QK), half),
            pltpu.VMEM((rows, PAIR_V), half),
            pltpu.SemaphoreType.DMA((10, pairs)),
            pltpu.SemaphoreType.DMA((10, pairs)),
        ],
        compiler_params=pltpu.CompilerParams(
            collective_id=0, has_side_effects=True, vmem_limit_bytes=58 * 2**20
        ),
        name="window_grads",
    )(
        queries[0],
        key_states[0],
        value_states[0],
        out_grad[0],
        lse_rest[0].reshape(pairs, 2, rows),
        out_dot[0].reshape(pairs, 2, rows),
    )
    return [out[None] for out in outs]


def passed_along(x, axis, by):
    length = lax.axis_size(axis)
    return lax.ppermute(x, axis, [(i, (i + by) % length) for i in range(length)])


def expert_part(moe_acts, moe_grads, counts, replica_list):
    acts = moe_acts[0]
    grads = moe_grads[0]
    group = lax.axis_index("grp")
    groups = lax.axis_size("grp")
    replicas = replica_list.shape[1]
    own = acts.shape[0] - replicas
    acts_in = [acts[slot] for slot in range(own)]
    grads_in = [grads[slot] for slot in range(own)]
    live = [counts[group, slot] for slot in range(own)]
    expert = [jnp.int32(slot) for slot in range(own)]
    for replica in range(replicas):
        source = (group - 1 - replica) % groups
        acts_in.append(passed_along(acts[own + replica], "grp", replica + 1))
        grads_in.append(passed_along(grads[own + replica], "grp", replica + 1))
        live.append(counts[source, own + replica])
        expert.append(replica_list[source, replica])
    rows_all = lax.all_gather(jnp.stack(grads_in), "ctx", axis=1, tiled=True)
    row_ids = lax.iota(jnp.int32, rows_all.shape[1])
    keep = row_ids[None, :] < jnp.stack(live)[:, None]
    chosen = jnp.stack(expert)[:, None] == lax.iota(jnp.int32, own)[None, :]
    parts = []
    left = jnp.concatenate(acts_in, 1)
    for k in range(own):
        masked = jnp.where((keep & chosen[:, k : k + 1])[:, :, None], rows_all, jnp.zeros_like(rows_all))
        parts.append(
            jnp.dot(left, masked.reshape(-1, masked.shape[2]), preferred_element_type=jnp.float32)
        )
    return jnp.stack(parts)[None]


def local(queries, key_states, value_states, out_grad, lse_rest, out_dot, moe_acts, moe_grads, counts, replica_list):
    grads = attention_part(queries, key_states, value_states, out_grad, lse_rest, out_dot)
    expert_grad = expert_part(moe_acts, moe_grads, counts, replica_list)
    return (*grads, expert_grad)


def solution(mesh):
    return jax.shard_map(
        local,
        mesh=mesh,
        in_specs=(
            P("grp", "ctx", None),
            P("grp", "ctx", None),
            P("grp", "ctx", None),
            P("grp", "ctx", None),
            P("grp", None, "ctx"),
            P("grp", None, "ctx"),
            P("grp", None, "ctx", None),
            P("grp", None, "ctx", None),
            P(),
            P(),
        ),
        out_specs=(
            P("grp", "ctx", None),
            P("grp", "ctx", None),
            P("grp", "ctx", None),
            P("grp", None, "ctx", None),
        ),
        check_vma=False,
    )
```

time: 746 us -> 326 us (0.44)
  the two profiles are of different devices: /device:TPU:26 before, /device:TPU:3 now
where the time goes in v1:
time: 326 us; the launch traced here: 325 us
  Pallas kernels  223 us (68%)
  starting transfers between devices  33.7 us (10%)
  local copies, waits for them, and re-layouts  33.2 us (10%)
  between operations  14.2 us (4%)
  matrix products  7.81 us (2%)
  waiting for transfers between devices  7.61 us (2%)
  other arithmetic  5.79 us (2%)
    pallas_call x1, Pallas kernels, attention_part(): pl.pallas_call(functools.partial(attention_kernel, pairs), out_shape=[jax...  223 us
    ppermute x14, starting transfers between devices, passed_along(): lax.ppermute(x, axis, [(i, (i + by) % length) for i in range(length)])  33.6 us
    unnamed x35, local copies, waits for them, and re-layouts  17.8 us
    dot_general x2, matrix products, expert_part(): jnp.dot(left, masked.reshape(-1, masked.shape[2]), preferred_element_type...  7.81 us
    ppermute x14, waiting for transfers between devices, passed_along(): lax.ppermute(x, axis, [(i, (i + by) % length) for i in range(length)])  7.59 us
  transfers between devices with their start and end apart: 15, of which 3 were waited for; matrix products, arithmetic and copies ran while one was open for 7% of the time, Pallas kernels for 69%

profile of v1, /device:TPU:3, one launch (start us, length us, event | category | flops | bytes accessed | tf_op | source)
XLA Modules:
  0.0 324.9 jit_solution(12141981000717165278)
XLA Ops:
  7.2 0.9 slice_bitcast_fusion.7
  8.1 3.7 %collective-permute-start.7 = (bf16[16,1024]{1,0:T(8,128)(2,1)S(1)}, bf16[16,1024]{1,0:T(8,128)(2,1)S(1)}, u32[]{:S(2)}, u32[]{:S(2)}) collective-permute-start(bf16[16,1024]{1,0:T(8,128)(2,1)S(1)} %get-tuple-element.24), channel_id=1, source_target_pairs={{0,1},{1,2},{2,3},{3,4},{4,5},{5,6},{6,7},{7,0},{8,9},{9,10},{10,1... | collective-permute-start | bytes 98312 | tf_op jit(solution)/shard_map/ppermute | solution.py:388
  11.8 1.3 collective-permute-start.8
  13.1 1.1 collective-permute-start.9
  14.2 1.6 collective-permute-start.10
  15.7 5.3 %collective-permute-start.11 = (bf16[16,1024]{1,0:T(8,128)(2,1)S(1)}, bf16[16,1024]{1,0:T(8,128)(2,1)S(1)}, u32[]{:S(2)}, u32[]{:S(2)}) collective-permute-start(bf16[16,1024]{1,0:T(8,128)(2,1)S(1)} %get-tuple-element.20), channel_id=1, source_target_pairs={{0,5},{1,6},{2,7},{3,0},{4,1},{5,2},{6,3},{7,4},{8,13},{9,14},{10,... | collective-permute-start | bytes 98312 | tf_op jit(solution)/shard_map/ppermute | solution.py:388
  21.0 0.8 constant_dynamic-update-slice_fusion.15
  22.6 1.1 collective-permute-start.12
  23.8 1.5 collective-permute-done.12
  25.3 2.7 collective-permute-done.13
  28.8 1.6 slice_bitcast_fusion
  30.9 2.8 collective-permute-start.2
  33.7 3.4 %collective-permute-start.3 = (bf16[448,256]{1,0:T(8,128)(2,1)S(1)}, bf16[448,256]{1,0:T(8,128)(2,1)S(1)}, u32[]{:S(2)}, u32[]{:S(2)}) collective-permute-start(bf16[448,256]{1,0:T(8,128)(2,1)S(1)} %get-tuple-element.14), channel_id=1, source_target_pairs={{0,4},{1,5},{2,6},{3,7},{4,0},{5,1},{6,2},{7,3},{8,12},{9,13},{10,... | collective-permute-start | bytes 688136 | tf_op jit(solution)/shard_map/ppermute | solution.py:388
  37.1 2.5 collective-permute-start.4
  40.4 4.5 %stack.40 = s32[9]{0:T(128)S(1)} concatenate(s32[1]{0:T(128)} %constant.78.clone.1, s32[1]{0:T(128)} %constant.79.clone.1, s32[1]{0:T(128)} %bitcast.25, s32[1]{0:T(128)} %bitcast.26, s32[1]{0:T(128)} %bitcast.27, s32[1]{0:T(128)} %bitcast.28, s32[1]{0:T(128)} %bitcast.29, s32[1]{0:T(128)} %bitcast.30, s32[1]{0:T(128)} %bitcast.31), dimensions={0} | concatenate | bytes 72 | tf_op jit(solution)/shard_map/stack | solution.py:411
  44.9 1.6 bitcast_dynamic-update-slice_fusion.1
  46.6 1.6 bitcast_dynamic-update-slice_fusion
  48.2 5.7 %stack.39 = s32[9]{0:T(128)S(1)} concatenate(s32[1]{0:T(128)} %bitcast.16, s32[1]{0:T(128)} %bitcast.17, s32[1]{0:T(128)} %bitcast.18, s32[1]{0:T(128)} %bitcast.19, s32[1]{0:T(128)} %bitcast.20, s32[1]{0:T(128)} %bitcast.21, s32[1]{0:T(128)} %bitcast.22, s32[1]{0:T(128)} %bitcast.23, s32[1]{0:T(128)} %bitcast.24), dimensions={0} | concatenate | bytes 72 | tf_op jit(solution)/shard_map/stack | solution.py:410
  55.3 222.6 %window_grads.1 = (bf16[256,6144]{1,0:T(8,128)(2,1)}, bf16[256,6144]{1,0:T(8,128)(2,1)}, bf16[256,4096]{1,0:T(8,128)(2,1)}) custom-call(bf16[256,6144]{1,0:T(8,128)(2,1)} %bitcast.93, bf16[256,6144]{1,0:T(8,128)(2,1)} %bitcast.94, bf16[256,4096]{1,0:T(8,128)(2,1)} %bitcast.95, bf16[256,4096]{1,0:T(8,128)(2,1)} %bitcast.96, ...), custom_call_target="tpu_custom_call" | custom-call | tf_op jit(solution)/shard_map/window_grads/pallas_call | solution.py:338
  277.9 7.4 %collective-permute-start.5 = (bf16[448,256]{1,0:T(8,128)(2,1)S(1)}, bf16[448,256]{1,0:T(8,128)(2,1)S(1)}, u32[]{:S(2)}, u32[]{:S(2)}) collective-permute-start(bf16[448,256]{1,0:T(8,128)(2,1)S(1)} %get-tuple-element.18), channel_id=1, source_target_pairs={{0,6},{1,7},{2,0},{3,1},{4,2},{5,3},{6,4},{7,5},{8,14},{9,15},{10,... | collective-permute-start | bytes 688136 | tf_op jit(solution)/shard_map/ppermute | solution.py:388
  286.1 2.8 collective-permute-start.6
  292.4 3.4 %collective-permute-done.6 = bf16[448,256]{1,0:T(8,128)(2,1)S(1)} collective-permute-done((bf16[448,256]{1,0:T(8,128)(2,1)S(1)}, bf16[448,256]{1,0:T(8,128)(2,1)S(1)}, u32[]{:S(2)}, u32[]{:S(2)}) %collective-permute-start.6) | collective-permute-done | bytes 229408 | tf_op jit(solution)/shard_map/ppermute | solution.py:388
  296.5 3.4 %broadcast_select_fusion.1 = (bf16[9,256,1024]{2,1,0:T(8,128)(2,1)S(1)}, bf16[9,256,1024]{2,1,0:T(8,128)(2,1)S(1)}) fusion(bf16[9,256,1024]{2,1,0:T(8,128)(2,1)} %all-gather.2.cloned.1.call-done, pred[9,256]{1,0:T(8,128)(4,1)S(1)} %get-tuple-element.42, pred[9,256]{1,0:T(8,128)(4,1)S(1)} %get-tuple-element.43), kind=kLoop, calls=%fused_computation.1 | loop fusion | flops 4718592 | bytes 14160384 | tf_op jit(solution)/shard_map/jit(_where)/select_n | solution.py:415
  300.0 3.9 %convolution_bitcast_fusion.1 = f32[1,448,1024]{2,1,0:T(8,128)S(1)} fusion(bf16[448,2304]{1,0:T(8,128)(2,1)} %constant_dynamic-update-slice_fusion, bf16[2304,1024]{1,0:T(8,128)(2,1)S(1)} %bitcast.90), kind=kOutput, calls=%fused_computation.4 | convolution fusion | flops 2113929216 | bytes 8617984 | tf_op jit(solution)/shard_map/dot_general | solution.py:417
  303.9 3.9 %convolution_bitcast_fusion = f32[1,448,1024]{2,1,0:T(8,128)S(1)} fusion(bf16[448,2304]{1,0:T(8,128)(2,1)} %constant_dynamic-update-slice_fusion, bf16[2304,1024]{1,0:T(8,128)(2,1)S(1)} %bitcast.89), kind=kOutput, calls=%fused_computation.3 | convolution fusion | flops 2113929216 | bytes 8617984 | tf_op jit(solution)/shard_map/dot_general | solution.py:417
  307.8 2.3 maximum_bitcast_fusion
  310.1 0.9 copy-done.1
  311.0 1.7 copy.33
  312.7 1.4 copy-done
  314.0 1.7 copy.34
  315.7 1.1 copy-done.2
  316.8 1.3 copy.35
  (51 shorter events, 9.2 us)
Async XLA Ops:
  7.2 289.4 %all-gather.2.cloned.1.call-start = ((), (), s32[]{:S(2)}) async-start(), calls=%async_computation | async-start | bytes 5013504 | tf_op jit(solution)/shard_map/all_gather | solution.py:408
  8.1 14.5 %collective-permute-start.7 = (bf16[16,1024]{1,0:T(8,128)(2,1)S(1)}, bf16[16,1024]{1,0:T(8,128)(2,1)S(1)}, u32[]{:S(2)}, u32[]{:S(2)}) collective-permute-start(bf16[16,1024]{1,0:T(8,128)(2,1)S(1)} %get-tuple-element.24), channel_id=1, source_target_pairs={{0,1},{1,2},{2,3},{3,4},{4,5},{5,6},{6,7},{7,0},{8,9},{9,10},{10,1... | collective-permute-start | bytes 98312 | tf_op jit(solution)/shard_map/ppermute | solution.py:388
  11.8 11.9 %collective-permute-start.8 = (bf16[16,1024]{1,0:T(8,128)(2,1)S(1)}, bf16[16,1024]{1,0:T(8,128)(2,1)S(1)}, u32[]{:S(2)}, u32[]{:S(2)}) collective-permute-start(bf16[16,1024]{1,0:T(8,128)(2,1)S(1)} %get-tuple-element.23), channel_id=1, source_target_pairs={{0,2},{1,3},{2,4},{3,5},{4,6},{5,7},{6,0},{7,1},{8,10},{9,11},{10,... | collective-permute-start | bytes 98312 | tf_op jit(solution)/shard_map/ppermute | solution.py:388
  13.1 10.7 %collective-permute-start.9 = (bf16[16,1024]{1,0:T(8,128)(2,1)S(1)}, bf16[16,1024]{1,0:T(8,128)(2,1)S(1)}, u32[]{:S(2)}, u32[]{:S(2)}) collective-permute-start(bf16[16,1024]{1,0:T(8,128)(2,1)S(1)} %get-tuple-element.22), channel_id=1, source_target_pairs={{0,3},{1,4},{2,5},{3,6},{4,7},{5,0},{6,1},{7,2},{8,11},{9,12},{10,... | collective-permute-start | bytes 98312 | tf_op jit(solution)/shard_map/ppermute | solution.py:388
  14.2 9.6 %collective-permute-start.10 = (bf16[16,1024]{1,0:T(8,128)(2,1)S(1)}, bf16[16,1024]{1,0:T(8,128)(2,1)S(1)}, u32[]{:S(2)}, u32[]{:S(2)}) collective-permute-start(bf16[16,1024]{1,0:T(8,128)(2,1)S(1)} %get-tuple-element.21), channel_id=1, source_target_pairs={{0,4},{1,5},{2,6},{3,7},{4,0},{5,1},{6,2},{7,3},{8,12},{9,13},{10,... | collective-permute-start | bytes 98312 | tf_op jit(solution)/shard_map/ppermute | solution.py:388
  15.7 8.1 %collective-permute-start.11 = (bf16[16,1024]{1,0:T(8,128)(2,1)S(1)}, bf16[16,1024]{1,0:T(8,128)(2,1)S(1)}, u32[]{:S(2)}, u32[]{:S(2)}) collective-permute-start(bf16[16,1024]{1,0:T(8,128)(2,1)S(1)} %get-tuple-element.20), channel_id=1, source_target_pairs={{0,5},{1,6},{2,7},{3,0},{4,1},{5,2},{6,3},{7,4},{8,13},{9,14},{10,... | collective-permute-start | bytes 98312 | tf_op jit(solution)/shard_map/ppermute | solution.py:388
  22.6 2.8 collective-permute-start.12
  23.6 16.0 %copy-start.6 = (s32[8,9]{1,0:T(8,128)S(1)}, s32[8,9]{1,0:T(8,128)}, u32[]{:S(2)}) copy-start(s32[8,9]{1,0:T(8,128)} %param.18) | copy-start | bytes 868
  23.7 16.0 %copy-start.7 = (s32[8,7]{1,0:T(8,128)S(1)}, s32[8,7]{1,0:T(8,128)}, u32[]{:S(2)}) copy-start(s32[8,7]{1,0:T(8,128)} %param.19) | copy-start | bytes 676
  23.7 4.3 %collective-permute-start.13 = (bf16[16,1024]{1,0:T(8,128)(2,1)S(1)}, bf16[16,1024]{1,0:T(8,128)(2,1)S(1)}, u32[]{:S(2)}, u32[]{:S(2)}) collective-permute-start(bf16[16,1024]{1,0:T(8,128)(2,1)S(1)} %get-tuple-element.19), channel_id=1, source_target_pairs={{0,7},{1,0},{2,1},{3,2},{4,3},{5,4},{6,5},{7,6},{8,15},{9,8},{10,9... | collective-permute-start | bytes 98312 | tf_op jit(solution)/shard_map/ppermute | solution.py:388
  28.0 0.7 copy-start.3
  28.7 25.3 %copy-start.4 = (f32[1,32,256]{2,1,0:T(8,128)S(1)}, f32[1,32,256]{2,1,0:T(8,128)}, u32[]{:S(2)}) copy-start(f32[1,32,256]{2,1,0:T(8,128)} %param.14) | copy-start | bytes 98308
  28.8 25.9 %copy-start.5 = (f32[1,32,256]{2,1,0:T(8,128)S(1)}, f32[1,32,256]{2,1,0:T(8,128)}, u32[]{:S(2)}) copy-start(f32[1,32,256]{2,1,0:T(8,128)} %param.15) | copy-start | bytes 98308
  30.4 247.6 %collective-permute-start = (bf16[448,256]{1,0:T(8,128)(2,1)S(1)}, bf16[448,256]{1,0:T(8,128)(2,1)S(1)}, u32[]{:S(2)}, u32[]{:S(2)}) collective-permute-start(bf16[448,256]{1,0:T(8,128)(2,1)S(1)} %get-tuple-element.17), channel_id=1, source_target_pairs={{0,1},{1,2},{2,3},{3,4},{4,5},{5,6},{6,7},{7,0},{8,9},{9,10},{10,1... | collective-permute-start | bytes 688136 | tf_op jit(solution)/shard_map/ppermute | solution.py:388
  30.8 255.3 %collective-permute-start.1 = (bf16[448,256]{1,0:T(8,128)(2,1)S(1)}, bf16[448,256]{1,0:T(8,128)(2,1)S(1)}, u32[]{:S(2)}, u32[]{:S(2)}) collective-permute-start(bf16[448,256]{1,0:T(8,128)(2,1)S(1)} %get-tuple-element.16), channel_id=1, source_target_pairs={{0,2},{1,3},{2,4},{3,5},{4,6},{5,7},{6,0},{7,1},{8,10},{9,11},{10,... | collective-permute-start | bytes 688136 | tf_op jit(solution)/shard_map/ppermute | solution.py:388
  30.9 258.7 %collective-permute-start.2 = (bf16[448,256]{1,0:T(8,128)(2,1)S(1)}, bf16[448,256]{1,0:T(8,128)(2,1)S(1)}, u32[]{:S(2)}, u32[]{:S(2)}) collective-permute-start(bf16[448,256]{1,0:T(8,128)(2,1)S(1)} %get-tuple-element.15), channel_id=1, source_target_pairs={{0,3},{1,4},{2,5},{3,6},{4,7},{5,0},{6,1},{7,2},{8,11},{9,12},{10,... | collective-permute-start | bytes 688136 | tf_op jit(solution)/shard_map/ppermute | solution.py:388
  33.7 256.6 %collective-permute-start.3 = (bf16[448,256]{1,0:T(8,128)(2,1)S(1)}, bf16[448,256]{1,0:T(8,128)(2,1)S(1)}, u32[]{:S(2)}, u32[]{:S(2)}) collective-permute-start(bf16[448,256]{1,0:T(8,128)(2,1)S(1)} %get-tuple-element.14), channel_id=1, source_target_pairs={{0,4},{1,5},{2,6},{3,7},{4,0},{5,1},{6,2},{7,3},{8,12},{9,13},{10,... | collective-permute-start | bytes 688136 | tf_op jit(solution)/shard_map/ppermute | solution.py:388
  37.1 253.9 %collective-permute-start.4 = (bf16[448,256]{1,0:T(8,128)(2,1)S(1)}, bf16[448,256]{1,0:T(8,128)(2,1)S(1)}, u32[]{:S(2)}, u32[]{:S(2)}) collective-permute-start(bf16[448,256]{1,0:T(8,128)(2,1)S(1)} %get-tuple-element.13), channel_id=1, source_target_pairs={{0,5},{1,6},{2,7},{3,0},{4,1},{5,2},{6,3},{7,4},{8,13},{9,14},{10,... | collective-permute-start | bytes 688136 | tf_op jit(solution)/shard_map/ppermute | solution.py:388
  277.9 13.8 %collective-permute-start.5 = (bf16[448,256]{1,0:T(8,128)(2,1)S(1)}, bf16[448,256]{1,0:T(8,128)(2,1)S(1)}, u32[]{:S(2)}, u32[]{:S(2)}) collective-permute-start(bf16[448,256]{1,0:T(8,128)(2,1)S(1)} %get-tuple-element.18), channel_id=1, source_target_pairs={{0,6},{1,7},{2,0},{3,1},{4,2},{5,3},{6,4},{7,5},{8,14},{9,15},{10,... | collective-permute-start | bytes 688136 | tf_op jit(solution)/shard_map/ppermute | solution.py:388
  286.1 9.7 %collective-permute-start.6 = (bf16[448,256]{1,0:T(8,128)(2,1)S(1)}, bf16[448,256]{1,0:T(8,128)(2,1)S(1)}, u32[]{:S(2)}, u32[]{:S(2)}) collective-permute-start(bf16[448,256]{1,0:T(8,128)(2,1)S(1)} %get-tuple-element.12), channel_id=1, source_target_pairs={{0,7},{1,0},{2,1},{3,2},{4,3},{5,4},{6,5},{7,6},{8,15},{9,8},{10,9... | collective-permute-start | bytes 688136 | tf_op jit(solution)/shard_map/ppermute | solution.py:388
  307.8 3.2 copy-start.1
  311.0 3.0 copy-start
  314.0 2.7 copy-start.2
Sparse Core Ops, SparseCore 0:
  28.9 50.6 all-gather.1

commit v2 on v1

--- a/solution.py
+++ b/solution.py
@@ -11,12 +11,31 @@
 V_DIM = 128
 PAIR_QK = 2 * QK_DIM
 PAIR_V = 2 * V_DIM
-AHEAD = 3
+AHEAD = 1
 SCALE = QK_DIM**-0.5
 LOW = -1e38
 MESH = pl.DeviceIdType.MESH
 
 M_Q, M_G, M_K, M_V, M_DQ, M_MS, M_W, M_DK, M_DV, M_DOT = range(10)
+
+E_ACTS, E_ROWS, E_HIGH, E_SPREAD, E_LEVEL, E_AROUND, E_OTHER = range(7)
+
+
+def first_sems(replicas, owners, columns):
+    sizes = {
+        E_ACTS: replicas,
+        E_ROWS: replicas,
+        E_HIGH: 1,
+        E_SPREAD: 2 * (owners - 1),
+        E_LEVEL: 1,
+        E_AROUND: 2 * (columns - 1),
+        E_OTHER: 2 * columns,
+    }
+    starts, total = {}, 0
+    for kind, size in sizes.items():
+        starts[kind] = total
+        total += size
+    return starts, total
 
 
 def rows_by_rows(a, b):
@@ -57,9 +76,14 @@
     g,
     rest,
     dot,
+    acts,
+    high,
+    pieces,
+    lanes,
     dq,
     dk,
     dv,
+    expert,
     qn,
     gn,
     dotn,
@@ -80,8 +104,15 @@
     accv,
     q2,
     g2,
+    left,
+    right,
+    made,
     send,
     recv,
+    esend,
+    erecv,
+    own_sem,
+    out_sem,
 ):
     rows = q.shape[0]
     me = lax.axis_index("ctx")
@@ -123,10 +154,180 @@
             device_id_type=MESH,
         )
 
+    group = lax.axis_index("grp")
+    groups = lax.axis_size("grp")
+    slots = acts.shape[0]
+    replicas = groups - 1
+    own_slots = slots - replicas
+    half_rows = left.shape[1] // (2 * slots)
+    piece = pieces.shape[1]
+    columns = total // 4
+    owners = groups // 2
+    upper = (me >= total // 2).astype(jnp.int32)
+    level = me + 2 - 4 * (lax.rem(me, 4) // 2)
+    twin = group + 1 - 2 * lax.rem(group, 2)
+    starts, _ = first_sems(replicas, owners, columns)
+
+    def unit(device):
+        return right.at[
+            pl.ds(slots * (device >= total // 2).astype(jnp.int32), slots),
+            pl.ds(pl.multiple_of(lax.rem(device, total // 2) * piece, piece), piece),
+        ]
+
+    def block(index):
+        return left.at[:, pl.ds(pl.multiple_of(index * half_rows, 128), half_rows)]
+
+    def expert_message(kind, at, src, dst, target):
+        sem = starts[kind] + at
+        return pltpu.make_async_remote_copy(
+            src_ref=src,
+            dst_ref=dst,
+            send_sem=esend.at[sem],
+            recv_sem=erecv.at[sem],
+            device_id=target,
+            device_id_type=MESH,
+        )
+
+    def in_group(device):
+        return {"ctx": device, "grp": group}
+
+    def owner(index):
+        return {"ctx": me, "grp": index}
+
+    def expert_messages(kind):
+        if kind == E_ACTS:
+            return [
+                expert_message(
+                    kind,
+                    r,
+                    acts.at[own_slots + r, :, pl.ds(0, half_rows)],
+                    block(own_slots + r),
+                    owner(lax.rem(group + r + 1, groups)),
+                )
+                for r in range(replicas)
+            ]
+        if kind == E_ROWS:
+            return [
+                expert_message(
+                    kind,
+                    r,
+                    pieces.at[own_slots + r],
+                    right.at[
+                        slots * upper + own_slots + r,
+                        pl.ds(pl.multiple_of(lax.rem(me, total // 2) * piece, piece), piece),
+                    ],
+                    owner(lax.rem(group + r + 1, groups)),
+                )
+                for r in range(replicas)
+            ]
+        if kind == E_HIGH:
+            place = lax.rem(twin - group + groups, groups)
+            return [expert_message(kind, 0, high, block(slots + 1 + place), owner(twin))]
+        if kind == E_SPREAD:
+            place = lax.rem(group - twin + groups, groups)
+            found = []
+            for m in range(1, owners):
+                to = owner(lax.rem(group + 2 * m, groups))
+                found.append(
+                    expert_message(kind, 2 * m - 2, high, block(slots + 1 + 2 * m), to)
+                )
+                found.append(
+                    expert_message(
+                        kind,
+                        2 * m - 1,
+                        block(slots + 1 + place),
+                        block(slots + 1 + lax.rem(place + 2 * m, groups)),
+                        to,
+                    )
+                )
+            return found
+        if kind == E_LEVEL:
+            return [expert_message(kind, 0, unit(me), unit(me), in_group(level))]
+        if kind == E_AROUND:
+            return [
+                expert_message(
+                    kind,
+                    2 * m - 2 + which,
+                    unit(device),
+                    unit(device),
+                    in_group(lax.rem(me + 4 * m, total)),
+                )
+                for m in range(1, columns)
+                for which, device in enumerate((me, level))
+            ]
+        return [
+            expert_message(kind, m, unit(2 * m + core), unit(2 * m + core), in_group(other))
+            for m in range(2 * columns)
+        ]
+
+    def own_copies():
+        found = [
+            pltpu.make_async_copy(
+                acts.at[slot, :, pl.ds(0, half_rows)], block(slot), own_sem.at[slot]
+            )
+            for slot in range(own_slots)
+        ]
+        found.append(pltpu.make_async_copy(high, block(slots + 1), own_sem.at[own_slots]))
+        place = pl.ds(pl.multiple_of(lax.rem(me, total // 2) * piece, piece), piece)
+        for slot in range(own_slots):
+            found.append(
+                pltpu.make_async_copy(
+                    pieces.at[slot],
+                    right.at[slots * upper + slot, place],
+                    own_sem.at[own_slots + 1 + slot],
+                )
+            )
+        return found
+
+    def begin(*kinds):
+        for kind in kinds:
+            for each in expert_messages(kind):
+                each.start()
+
+    def arrived(*kinds):
+        for kind in kinds:
+            for each in expert_messages(kind):
+                each.wait_recv()
+
+    def left_behind(*kinds):
+        for kind in kinds:
+            for each in expert_messages(kind):
+                each.wait_send()
+
+    width = made.shape[2]
+    parts = right.shape[2] // width
+
+    def made_copy(index):
+        slot = lax.rem(index, 2)
+        cols = pl.ds(pl.multiple_of(lax.rem(index, parts) * width, 128), width)
+        return pltpu.make_async_copy(
+            made.at[slot], expert.at[lax.div(index, parts), :, cols], out_sem.at[slot]
+        )
+
+    def expert_step(index):
+        @pl.when(index >= 2)
+        def _():
+            made_copy(index - 2).wait()
+
+        mask = lanes[lax.div(index, parts)]
+        cols = pl.ds(pl.multiple_of(lax.rem(index, parts) * width, 128), width)
+        result = None
+        for low, count in ((0, slots), (slots + 1, slots - 1)):
+            here = slice(low * half_rows, (low + count) * half_rows)
+            a = left[:, here] * mask[:, here]
+            b = right[low : low + count, :, cols].reshape(count * half_rows, width)
+            product = plain(a, b)
+            result = product if result is None else result + product
+        made[lax.rem(index, 2)] = result
+        made_copy(index).start()
+
     barrier = pltpu.get_barrier_semaphore()
-    for partner in (behind_chip, ahead_chip, other):
-        pl.semaphore_signal(barrier, inc=1, device_id={"ctx": partner}, device_id_type=MESH)
-    pl.semaphore_wait(barrier, 3)
+    partners = [in_group(partner) for partner in (behind_chip, ahead_chip, other, level)]
+    partners += [in_group(lax.rem(me + 4 * m, total)) for m in range(1, columns)]
+    partners += [owner(lax.rem(group + m, groups)) for m in range(1, groups)]
+    for partner in partners:
+        pl.semaphore_signal(barrier, inc=1, device_id=partner, device_id_type=MESH)
+    pl.semaphore_wait(barrier, len(partners))
 
     message(M_DOT, 0).start()
     for pair in range(min(AHEAD, pairs)):
@@ -314,7 +515,50 @@
 
         return carry
 
-    lax.fori_loop(0, pairs + 3, step, 0)
+    def first_stage():
+        for each in own_copies():
+            each.start()
+        begin(E_ROWS, E_HIGH)
+
+    def second_stage():
+        begin(E_ACTS)
+
+    def third_stage():
+        for each in own_copies():
+            each.wait()
+        arrived(E_ROWS, E_HIGH)
+        begin(E_LEVEL, E_SPREAD)
+
+    def fourth_stage():
+        arrived(E_LEVEL)
+        begin(E_AROUND)
+
+    def fifth_stage():
+        arrived(E_AROUND)
+        begin(E_OTHER)
+
+    def sixth_stage():
+        arrived(E_OTHER, E_ACTS, E_SPREAD)
+
+    stages = {1: first_stage, 2: second_stage, 3: third_stage, 5: fourth_stage, 8: fifth_stage, 9: sixth_stage}
+    products = own_slots * parts
+    product_at = 10
+
+    def step_with_experts(at, carry):
+        step(at, carry)
+        for when, stage in stages.items():
+            pl.when(at == when)(stage)
+
+        @pl.when((at >= product_at) & (at < product_at + products))
+        def _():
+            expert_step(at - product_at)
+
+        return carry
+
+    lax.fori_loop(0, max(pairs + 3, product_at + products), step_with_experts, 0)
+    for index in range(products - 2, products):
+        made_copy(index).wait()
+    left_behind(E_ACTS, E_ROWS, E_HIGH, E_SPREAD, E_LEVEL, E_AROUND, E_OTHER)
 
     message(M_DOT, 0).wait_send()
 
@@ -326,24 +570,33 @@
     lax.fori_loop(0, pairs, drain, 0)
 
 
-def attention_part(queries, key_states, value_states, out_grad, lse_rest, out_dot):
-    rows, qk = queries.shape[1:]
-    vv = value_states.shape[2]
+def gradients(queries, key_states, value_states, out_grad, lse_rest, out_dot, acts, high, pieces, lanes):
+    rows, qk = queries.shape
+    vv = value_states.shape[1]
     pairs = qk // PAIR_QK
+    slots, features, cap = acts.shape
+    hidden = pieces.shape[2]
+    experts = lanes.shape[0]
+    groups = lax.axis_size("grp")
+    columns = lax.axis_size("ctx") // 4
+    width = min(hidden, 256)
+    _, sems = first_sems(groups - 1, groups // 2, columns)
     half = jnp.bfloat16
     vmem = pl.BlockSpec(memory_space=pltpu.VMEM)
+    anywhere = pl.BlockSpec(memory_space=pl.ANY)
     small = pltpu.VMEM((pairs, 8, rows), jnp.float32)
     wide = pltpu.VMEM((rows, qk), half)
     narrow = pltpu.VMEM((rows, vv), half)
-    outs = pl.pallas_call(
+    return pl.pallas_call(
         functools.partial(attention_kernel, pairs),
         out_shape=[
             jax.ShapeDtypeStruct((rows, qk), half),
             jax.ShapeDtypeStruct((rows, qk), half),
             jax.ShapeDtypeStruct((rows, vv), half),
+            jax.ShapeDtypeStruct((experts, features, hidden), jnp.float32),
         ],
-        in_specs=[vmem] * 6,
-        out_specs=[vmem] * 3,
+        in_specs=[vmem] * 6 + [anywhere] * 3 + [vmem],
+        out_specs=[vmem] * 3 + [anywhere],
         scratch_shapes=[
             wide,
             narrow,
@@ -365,64 +618,93 @@
             pltpu.VMEM((2, rows, PAIR_V), jnp.float32),
             pltpu.VMEM((rows, PAIR_QK), half),
             pltpu.VMEM((rows, PAIR_V), half),
+            pltpu.VMEM((features, slots * cap), half),
+            pltpu.VMEM((2 * slots, cap // 2, hidden), half),
+            pltpu.VMEM((2, features, width), jnp.float32),
             pltpu.SemaphoreType.DMA((10, pairs)),
             pltpu.SemaphoreType.DMA((10, pairs)),
+            pltpu.SemaphoreType.DMA((sems,)),
+            pltpu.SemaphoreType.DMA((sems,)),
+            pltpu.SemaphoreType.DMA((2 * experts + 1,)),
+            pltpu.SemaphoreType.DMA((2,)),
         ],
         compiler_params=pltpu.CompilerParams(
-            collective_id=0, has_side_effects=True, vmem_limit_bytes=58 * 2**20
+            collective_id=0, has_side_effects=True, vmem_limit_bytes=60 * 2**20
         ),
         name="window_grads",
     )(
+        queries,
+        key_states,
+        value_states,
+        out_grad,
+        lse_rest.reshape(pairs, 2, rows),
+        out_dot.reshape(pairs, 2, rows),
+        acts,
+        high,
+        pieces,
+        lanes,
+    )
+
+
+def expert_inputs(acts, grads, counts, replica_list):
+    group = lax.axis_index("grp")
+    groups = lax.axis_size("grp")
+    slots, _, cap = acts.shape
+    replicas = replica_list.shape[1]
+    own = slots - replicas
+    half_rows = cap // 2
+    full = jnp.argmax(counts[group])
+    high = lax.dynamic_slice(acts, (full, 0, half_rows), (1, acts.shape[1], half_rows))[0]
+    full_piece = lax.dynamic_slice_in_dim(grads, full, 1, 0)
+    upper = lax.axis_index("ctx") >= lax.axis_size("ctx") // 2
+    pieces = jnp.where(upper, jnp.broadcast_to(full_piece, grads.shape), grads)
+    block = lax.iota(jnp.int32, slots)
+    behind = jnp.maximum(block - own + 1, 0)
+    source = (group - behind) % groups
+    slot_id = lax.iota(jnp.int32, slots)
+    mine = (source[:, None] == lax.iota(jnp.int32, groups)[None, :]).astype(jnp.int32)
+    my_counts = jnp.sum(mine[:, :, None] * counts[None], 1)
+    my_lists = jnp.sum(mine[:, :, None] * replica_list[None], 1)
+    live = jnp.sum(jnp.where(block[:, None] == slot_id[None, :], my_counts, 0), 1)
+    listed = jnp.sum(
+        jnp.where((block[:, None] - own) == lax.iota(jnp.int32, replicas)[None, :], my_lists, 0), 1
+    )
+    expert = jnp.where(block < own, block, listed)
+    back = jnp.maximum(block - 1, 0)
+    src = (group - back) % groups
+    theirs = (src[:, None] == lax.iota(jnp.int32, groups)[None, :]).astype(jnp.int32)
+    their_counts = jnp.sum(theirs[:, :, None] * counts[None], 1)
+    their_full = jnp.argmax(their_counts, 1)
+    meant = jnp.where(back == 0, their_full < own, their_full == own + back - 1)
+    their_lists = jnp.sum(theirs[:, :, None] * replica_list[None], 1)
+    their_expert = jnp.sum(
+        jnp.where((their_full[:, None] - own) == lax.iota(jnp.int32, replicas)[None, :], their_lists, 0), 1
+    )
+    high_expert = jnp.where(back == 0, their_full, their_expert)
+    high_live = jnp.where(meant & (block >= 1), half_rows, 0)
+    all_live = jnp.concatenate([jnp.minimum(live, half_rows), high_live])
+    all_expert = jnp.concatenate([expert, high_expert])
+    wanted = all_expert[None] == lax.iota(jnp.int32, own)[:, None]
+    keep = lax.iota(jnp.int32, half_rows)[None, None] < jnp.where(wanted, all_live[None], 0)[:, :, None]
+    lanes = keep.astype(jnp.bfloat16).reshape(own, 1, 2 * slots * half_rows)
+    return high, pieces, lanes
+
+
+def local(queries, key_states, value_states, out_grad, lse_rest, out_dot, moe_acts, moe_grads, counts, replica_list):
+    high, pieces, lanes = expert_inputs(moe_acts[0], moe_grads[0], counts, replica_list)
+    found = gradients(
         queries[0],
         key_states[0],
         value_states[0],
         out_grad[0],
-        lse_rest[0].reshape(pairs, 2, rows),
-        out_dot[0].reshape(pairs, 2, rows),
+        lse_rest[0],
+        out_dot[0],
+        moe_acts[0],
+        high,
+        pieces,
+        lanes,
     )
-    return [out[None] for out in outs]
-
-
-def passed_along(x, axis, by):
-    length = lax.axis_size(axis)
-    return lax.ppermute(x, axis, [(i, (i + by) % length) for i in range(length)])
-
-
-def expert_part(moe_acts, moe_grads, counts, replica_list):
-    acts = moe_acts[0]
-    grads = moe_grads[0]
-    group = lax.axis_index("grp")
-    groups = lax.axis_size("grp")
-    replicas = replica_list.shape[1]
-    own = acts.shape[0] - replicas
-    acts_in = [acts[slot] for slot in range(own)]
-    grads_in = [grads[slot] for slot in range(own)]
-    live = [counts[group, slot] for slot in range(own)]
-    expert = [jnp.int32(slot) for slot in range(own)]
-    for replica in range(replicas):
-        source = (group - 1 - replica) % groups
-        acts_in.append(passed_along(acts[own + replica], "grp", replica + 1))
-        grads_in.append(passed_along(grads[own + replica], "grp", replica + 1))
-        live.append(counts[source, own + replica])
-        expert.append(replica_list[source, replica])
-    rows_all = lax.all_gather(jnp.stack(grads_in), "ctx", axis=1, tiled=True)
-    row_ids = lax.iota(jnp.int32, rows_all.shape[1])
-    keep = row_ids[None, :] < jnp.stack(live)[:, None]
-    chosen = jnp.stack(expert)[:, None] == lax.iota(jnp.int32, own)[None, :]
-    parts = []
-    left = jnp.concatenate(acts_in, 1)
-    for k in range(own):
-        masked = jnp.where((keep & chosen[:, k : k + 1])[:, :, None], rows_all, jnp.zeros_like(rows_all))
-        parts.append(
-            jnp.dot(left, masked.reshape(-1, masked.shape[2]), preferred_element_type=jnp.float32)
-        )
-    return jnp.stack(parts)[None]
-
-
-def local(queries, key_states, value_states, out_grad, lse_rest, out_dot, moe_acts, moe_grads, counts, replica_list):
-    grads = attention_part(queries, key_states, value_states, out_grad, lse_rest, out_dot)
-    expert_grad = expert_part(moe_acts, moe_grads, counts, replica_list)
-    return (*grads, expert_grad)
+    return tuple(each[None] for each in found)
 
 
 def solution(mesh):

time: 326 us -> 290 us (0.89)
  Pallas kernels: 223 us -> 263 us
  starting transfers between devices: 33.7 us -> 0 us
  local copies, waits for them, and re-layouts: 33.2 us -> 17.4 us
  between operations: 14.2 us -> 2.65 us
  matrix products: 7.81 us -> 0 us
  waiting for transfers between devices: 7.61 us -> 0 us
    pallas_call x1, Pallas kernels: 223 us -> 263 us  [gradients(): pl.pallas_call(functools.partial(attention_kernel, pairs), out_shape=[jax...]
    ppermute x14 -> x0, starting transfers between devices: 33.6 us -> none  [passed_along(): lax.ppermute(x, axis, [(i, (i + by) % length) for i in range(length)])]
    another operation x5 -> x2, local copies, waits for them, and re-layouts: 11.5 us -> 2.78 us  [the longest x1 1.39 us: gradients(): lse_rest.reshape(pairs, 2, rows)]
    dot_general x2 -> x0, matrix products: 7.81 us -> none  [expert_part(): jnp.dot(left, masked.reshape(-1, masked.shape[2]), preferred_element_type...]
    ppermute x14 -> x0, waiting for transfers between devices: 7.59 us -> none  [passed_along(): lax.ppermute(x, axis, [(i, (i + by) % length) for i in range(length)])]
    unnamed x35 -> x11, local copies, waits for them, and re-layouts: 17.8 us -> 12.2 us
  transfers between devices with their start and end apart: 15 -> 0, of which waited for: 3 -> 0; matrix products, arithmetic and copies ran while one was open for 7% -> 0% of each run, Pallas kernels for 69% -> 0%
where the time goes in v2:
time: 290 us; the launch traced here: 288 us
  Pallas kernels  263 us (91%)
  local copies, waits for them, and re-layouts  17.4 us (6%)
  other arithmetic  5.48 us (2%)
    pallas_call x1, Pallas kernels, gradients(): pl.pallas_call(functools.partial(attention_kernel, pairs), out_shape=[jax...  263 us
    unnamed x11, local copies, waits for them, and re-layouts  12.2 us

profile of v2, /device:TPU:3, one launch (start us, length us, event | category | flops | bytes accessed | tf_op | source)
XLA Modules:
  0.0 288.3 jit_solution(15881824137237728941)
XLA Ops:
  0.7 1.3 fusion.2
  4.0 0.8 copy.19
  4.7 0.1 fusion
  4.8 0.1 copy.18
  4.9 0.1 multiply_reduce_fusion.1
  5.0 0.8 multiply_reduce_fusion
  5.7 0.1 select_reduce_fusion
  5.9 0.6 iota_reduce_fusion
  6.5 0.1 pad_add_fusion
  6.6 0.1 lt.59
  6.7 0.6 compare_convert_fusion.lanes
  7.4 0.8 dynamic-slice_bitcast_fusion.1
  8.1 1.4 reshape_squeeze.6.rest
  9.5 1.4 reshape_squeeze.7.dot
  10.9 1.6 dynamic-slice_bitcast_fusion.high
  12.5 1.7 bitcast_select_fusion.pieces
  14.1 262.8 %window_grads.1 = (bf16[256,6144]{1,0:T(8,128)(2,1)}, bf16[256,6144]{1,0:T(8,128)(2,1)}, bf16[256,4096]{1,0:T(8,128)(2,1)}, f32[2,448,1024]{2,1,0:T(8,128)}) custom-call(bf16[256,6144]{1,0:T(8,128)(2,1)} %bitcast.24, bf16[256,6144]{1,0:T(8,128)(2,1)} %bitcast.25, bf16[256,4096]{1,0:T(8,128)(2,1)} %bitcast.28, bf16[256,4096]{1,0:T(8,128)(2,1)} %bitcast.29, ...), custom_call_target="tpu_custom_call" | custom-call | tf_op jit(solution)/shard_map/window_grads/pallas_call | solution.py:590
  276.9 0.0 copy-start.1
  277.0 4.0 %copy.26 = bf16[1,256,6144]{2,1,0:T(8,128)(2,1)} copy(bf16[1,256,6144]{2,1,0:T(8,128)(2,1)} %bitcast.23) | data formatting | bytes 6291456
  281.0 0.0 copy-done.1
  281.0 0.0 copy-start.2
  281.0 1.7 copy.27
  282.7 1.1 copy-done.2
  283.7 0.0 copy-start
  283.7 1.3 copy.28
  285.0 1.5 copy-done
  286.5 1.8 copy.29
  (10 shorter events, 0.1 us)
Async XLA Ops:
  276.9 4.0 %copy-start.1 = (bf16[256,6144]{1,0:T(8,128)(2,1)S(1)}, bf16[256,6144]{1,0:T(8,128)(2,1)}, u32[]{:S(2)}) copy-start(bf16[256,6144]{1,0:T(8,128)(2,1)} %get-tuple-element.13) | copy-start | bytes 9437188
  281.0 2.7 copy-start.2
  283.7 2.8 copy-start

commit v3 on v2

--- a/solution.py
+++ b/solution.py
@@ -11,12 +11,13 @@
 V_DIM = 128
 PAIR_QK = 2 * QK_DIM
 PAIR_V = 2 * V_DIM
-AHEAD = 1
 SCALE = QK_DIM**-0.5
 LOW = -1e38
 MESH = pl.DeviceIdType.MESH
 
 M_Q, M_G, M_K, M_V, M_DQ, M_MS, M_W, M_DK, M_DV, M_DOT = range(10)
+M_Q_VIA, M_G_VIA, M_DQ_VIA, M_Q_ON, M_G_ON, M_DQ_ON = range(10, 16)
+KINDS = 16
 
 E_ACTS, E_ROWS, E_HIGH, E_SPREAD, E_LEVEL, E_AROUND, E_OTHER = range(7)
 
@@ -84,6 +85,9 @@
     dk,
     dv,
     expert,
+    q_via,
+    g_via,
+    dq_via,
     qn,
     gn,
     dotn,
@@ -125,6 +129,29 @@
     c0 = jnp.where(core_zero, 1.0, 0.0).astype(jnp.float32)
     c1 = 1.0 - c0
     has_behind = me >= 2
+    has_ahead = me < total - 2
+    column = lax.div(me, 4)
+    low_level = lax.rem(me, 4) < 2
+    level = me + 2 - 4 * lax.div(lax.rem(me, 4), 2)
+    last_column = total // 4 - 1
+
+    def q_detour(boundary, pair):
+        return (lax.rem(pair, 4) <= boundary) & (pair >= 2)
+
+    def dq_detour(boundary, pair):
+        return lax.rem(pair, 4) < 3 - boundary
+
+    def sends_q_via(pair):
+        return low_level & (column >= 1) & q_detour(column - 1, pair)
+
+    def passes_q_on(pair):
+        return jnp.logical_not(low_level) & (column >= 1) & q_detour(column - 1, pair)
+
+    def sends_dq_via(pair):
+        return jnp.logical_not(low_level) & (column < last_column) & dq_detour(column, pair)
+
+    def passes_dq_on(pair):
+        return low_level & (column < last_column) & dq_detour(column, pair)
 
     def qk_cols(pair):
         return pl.ds(pl.multiple_of(pair * PAIR_QK, 128), PAIR_QK)
@@ -144,12 +171,31 @@
             M_DK: lambda: (dks.at[:, qk_cols(pair)], dk.at[:, qk_cols(pair)], other),
             M_DV: lambda: (dvs.at[:, v_cols(pair)], dv.at[:, v_cols(pair)], other),
             M_DOT: lambda: (dot, dotn, behind_chip),
+            M_Q_VIA: lambda: (q.at[:, qk_cols(pair)], q_via.at[:, qk_cols(pair)], level),
+            M_G_VIA: lambda: (g.at[:, v_cols(pair)], g_via.at[:, v_cols(pair)], level),
+            M_DQ_VIA: lambda: (dqs.at[:, qk_cols(pair)], dq_via.at[:, qk_cols(pair)], level),
+            M_Q_ON: lambda: (
+                q_via.at[:, qk_cols(pair)],
+                qn.at[:, qk_cols(pair)],
+                lax.rem(me + total - 4, total),
+            ),
+            M_G_ON: lambda: (
+                g_via.at[:, v_cols(pair)],
+                gn.at[:, v_cols(pair)],
+                lax.rem(me + total - 4, total),
+            ),
+            M_DQ_ON: lambda: (
+                dq_via.at[:, qk_cols(pair)],
+                dq.at[:, qk_cols(pair)],
+                lax.rem(me + 4, total),
+            ),
         }[kind]()
+        lands_as = {M_Q_ON: M_Q, M_G_ON: M_G, M_DQ_ON: M_DQ}.get(kind, kind)
         return pltpu.make_async_remote_copy(
             src_ref=src,
             dst_ref=dst,
             send_sem=send.at[kind, pair],
-            recv_sem=recv.at[kind, pair],
+            recv_sem=recv.at[lands_as, pair],
             device_id={"ctx": target},
             device_id_type=MESH,
         )
@@ -164,7 +210,6 @@
     columns = total // 4
     owners = groups // 2
     upper = (me >= total // 2).astype(jnp.int32)
-    level = me + 2 - 4 * (lax.rem(me, 4) // 2)
     twin = group + 1 - 2 * lax.rem(group, 2)
     starts, _ = first_sems(replicas, owners, columns)
 
@@ -329,10 +374,52 @@
         pl.semaphore_signal(barrier, inc=1, device_id=partner, device_id_type=MESH)
     pl.semaphore_wait(barrier, len(partners))
 
-    message(M_DOT, 0).start()
-    for pair in range(min(AHEAD, pairs)):
-        for kind in (M_Q, M_G, M_K, M_V):
-            message(kind, pair).start()
+    @pl.when(jnp.logical_not(has_ahead))
+    def _():
+        qn[...] = jnp.zeros_like(qn)
+        gn[...] = jnp.zeros_like(gn)
+        dotn[...] = jnp.zeros_like(dotn)
+        wr[...] = jnp.zeros_like(wr)
+
+    @pl.when(jnp.logical_not(has_behind))
+    def _():
+        msr[...] = jnp.zeros_like(msr)
+        dq[...] = jnp.zeros_like(dq)
+
+    def send_chunk(pair):
+        message(M_K, pair).start()
+        message(M_V, pair).start()
+        via = sends_q_via(pair)
+
+        @pl.when(has_behind & jnp.logical_not(via))
+        def _():
+            message(M_Q, pair).start()
+            message(M_G, pair).start()
+
+        @pl.when(via)
+        def _():
+            message(M_Q_VIA, pair).start()
+            message(M_G_VIA, pair).start()
+
+    def pass_q_on(pair):
+        @pl.when((pair < pairs) & passes_q_on(pair))
+        def _():
+            message(M_Q_VIA, pair).wait_recv()
+            message(M_Q_ON, pair).start()
+            message(M_G_VIA, pair).wait_recv()
+            message(M_G_ON, pair).start()
+
+    def pass_dq_on(pair):
+        @pl.when(passes_dq_on(pair))
+        def _():
+            message(M_DQ_VIA, pair).wait_recv()
+            message(M_DQ_ON, pair).start()
+
+    @pl.when(has_behind)
+    def _():
+        message(M_DOT, 0).start()
+
+    send_chunk(0)
 
     lane = lax.broadcasted_iota(jnp.int32, (1, 128), 1)
     low_lanes = jnp.where(lane < 64, 1.0, 0.0).astype(jnp.bfloat16)
@@ -354,17 +441,20 @@
         return ref[:, pl.ds(pl.multiple_of(pair * PAIR_V + head * V_DIM, 128), V_DIM)]
 
     def first_phase(pair):
-        for kind in (M_Q, M_G, M_K, M_V):
-            message(kind, pair).wait_recv()
-
-        @pl.when(pair == 0)
+        message(M_K, pair).wait_recv()
+        message(M_V, pair).wait_recv()
+
+        @pl.when(has_ahead)
+        def _():
+            message(M_Q, pair).wait_recv()
+            message(M_G, pair).wait_recv()
+
+        @pl.when((pair == 0) & has_ahead)
         def _():
             message(M_DOT, 0).wait_recv()
 
-        @pl.when(pair + AHEAD < pairs)
-        def _():
-            for kind in (M_Q, M_G, M_K, M_V):
-                message(kind, pair + AHEAD).start()
+        for extra, early in ((2 * pair + 1, True), (2 * pair + 2, True), (pair + 3, False)):
+            pl.when((extra < pairs) & ((pair < 2) == early))(functools.partial(send_chunk, extra))
 
         pick_second(pair)
         slot = lax.rem(pair, 3)
@@ -415,12 +505,42 @@
         zero = jnp.zeros((4, rows), jnp.float32)
         mss[pair] = jnp.concatenate(tops + sums + [zero], 0)
         own_ms[pair] = jnp.concatenate(tops_own + sums_own + [zero], 0)
-        message(M_MS, pair).start()
         store_pair(dqs, start, *dq_heads)
-        message(M_DQ, pair).start()
+        via = sends_dq_via(pair)
+
+        @pl.when(has_ahead)
+        def _():
+            message(M_MS, pair).start()
+
+        @pl.when(has_ahead & jnp.logical_not(via))
+        def _():
+            message(M_DQ, pair).start()
+
+        @pl.when(via)
+        def _():
+            message(M_DQ_VIA, pair).start()
+
+        @pl.when(pair == 1)
+        def _():
+            pass_q_on(1)
+            pass_q_on(2)
+
+        @pl.when(pair == 2)
+        def _():
+            pass_q_on(3)
+            pass_q_on(4)
+
+        @pl.when(pair >= 3)
+        def _():
+            pass_q_on(pair + 2)
 
     def second_phase(pair):
-        message(M_MS, pair).wait_recv()
+        pass_dq_on(pair)
+
+        @pl.when(has_behind)
+        def _():
+            message(M_MS, pair).wait_recv()
+
         theirs = msr[pair]
         ours = own_ms[pair]
         away = rest[pair]
@@ -435,11 +555,20 @@
         zero = jnp.zeros((6, rows), jnp.float32)
         ws[pair] = jnp.concatenate([jnp.exp(top_far - total_lse), zero], 0)
         fo[pair] = jnp.concatenate([jnp.exp(ours[0:2] - total_lse), zero], 0)
-        message(M_W, pair).start()
+
+        @pl.when(has_behind)
+        def _():
+            message(M_W, pair).start()
 
     def third_phase(pair):
-        message(M_W, pair).wait_recv()
-        message(M_DQ, pair).wait_recv()
+        @pl.when(has_ahead)
+        def _():
+            message(M_W, pair).wait_recv()
+
+        @pl.when(has_behind)
+        def _():
+            message(M_DQ, pair).wait_recv()
+
         pick_second(pair)
         slot = lax.rem(pair, 3)
         start = pl.multiple_of(pair * PAIR_QK, 128)
@@ -560,11 +689,26 @@
         made_copy(index).wait()
     left_behind(E_ACTS, E_ROWS, E_HIGH, E_SPREAD, E_LEVEL, E_AROUND, E_OTHER)
 
-    message(M_DOT, 0).wait_send()
+    @pl.when(has_behind)
+    def _():
+        message(M_DOT, 0).wait_send()
 
     def drain(pair, carry):
-        for kind in (M_Q, M_G, M_K, M_V, M_DQ, M_MS, M_W, M_DK, M_DV):
-            message(kind, pair).wait_send()
+        def settle(condition, *kinds):
+            @pl.when(condition)
+            def _():
+                for kind in kinds:
+                    message(kind, pair).wait_send()
+
+        settle(pair >= 0, M_K, M_V, M_DK, M_DV)
+        settle(has_behind, M_W)
+        settle(has_ahead, M_MS)
+        settle(has_behind & jnp.logical_not(sends_q_via(pair)), M_Q, M_G)
+        settle(sends_q_via(pair), M_Q_VIA, M_G_VIA)
+        settle(passes_q_on(pair), M_Q_ON, M_G_ON)
+        settle(has_ahead & jnp.logical_not(sends_dq_via(pair)), M_DQ)
+        settle(sends_dq_via(pair), M_DQ_VIA)
+        settle(passes_dq_on(pair), M_DQ_ON)
         return carry
 
     lax.fori_loop(0, pairs, drain, 0)
@@ -594,9 +738,12 @@
             jax.ShapeDtypeStruct((rows, qk), half),
             jax.ShapeDtypeStruct((rows, vv), half),
             jax.ShapeDtypeStruct((experts, features, hidden), jnp.float32),
+            jax.ShapeDtypeStruct((rows, qk), half),
+            jax.ShapeDtypeStruct((rows, vv), half),
+            jax.ShapeDtypeStruct((rows, qk), half),
         ],
         in_specs=[vmem] * 6 + [anywhere] * 3 + [vmem],
-        out_specs=[vmem] * 3 + [anywhere],
+        out_specs=[vmem] * 3 + [anywhere] * 4,
         scratch_shapes=[
             wide,
             narrow,
@@ -621,8 +768,8 @@
             pltpu.VMEM((features, slots * cap), half),
             pltpu.VMEM((2 * slots, cap // 2, hidden), half),
             pltpu.VMEM((2, features, width), jnp.float32),
-            pltpu.SemaphoreType.DMA((10, pairs)),
-            pltpu.SemaphoreType.DMA((10, pairs)),
+            pltpu.SemaphoreType.DMA((KINDS, pairs)),
+            pltpu.SemaphoreType.DMA((KINDS, pairs)),
             pltpu.SemaphoreType.DMA((sems,)),
             pltpu.SemaphoreType.DMA((sems,)),
             pltpu.SemaphoreType.DMA((2 * experts + 1,)),
@@ -643,7 +790,7 @@
         high,
         pieces,
         lanes,
-    )
+    )[:4]
 
 
 def expert_inputs(acts, grads, counts, replica_list):

time: 290 us -> 256 us (0.88)
  Pallas kernels: 263 us -> 230 us
    pallas_call x1, Pallas kernels: 263 us -> 230 us  [gradients(): pl.pallas_call(functools.partial(attention_kernel, pairs), out_shape=[jax...]
where the time goes in v3:
time: 256 us; the launch traced here: 255 us
  Pallas kernels  230 us (90%)
  local copies, waits for them, and re-layouts  17.4 us (7%)
  other arithmetic  5.48 us (2%)
  between operations  2.65 us (1%)
    pallas_call x1, Pallas kernels, gradients(): pl.pallas_call(functools.partial(attention_kernel, pairs), out_shape=[jax...  230 us
    unnamed x11, local copies, waits for them, and re-layouts  12.2 us

profile of v3, /device:TPU:3, one launch (start us, length us, event | category | flops | bytes accessed | tf_op | source)
XLA Modules:
  0.0 255.3 jit_solution(16943269288473562568)
XLA Ops:
  0.7 1.3 fusion.2
  4.0 0.8 copy.19
  4.7 0.1 fusion
  4.8 0.1 copy.18
  4.9 0.1 multiply_reduce_fusion.1
  5.0 0.8 multiply_reduce_fusion
  5.7 0.1 select_reduce_fusion
  5.9 0.6 iota_reduce_fusion
  6.5 0.1 pad_add_fusion
  6.6 0.1 lt.59
  6.7 0.6 compare_convert_fusion.lanes
  7.4 0.8 dynamic-slice_bitcast_fusion.1
  8.1 1.4 reshape_squeeze.6.rest
  9.5 1.4 reshape_squeeze.7.dot
  10.9 1.6 dynamic-slice_bitcast_fusion.high
  12.5 1.7 bitcast_select_fusion.pieces
  14.1 229.7 %window_grads.1 = (bf16[256,6144]{1,0:T(8,128)(2,1)}, bf16[256,6144]{1,0:T(8,128)(2,1)}, bf16[256,4096]{1,0:T(8,128)(2,1)}, f32[2,448,1024]{2,1,0:T(8,128)}, bf1...) custom-call(bf16[256,6144]{1,0:T(8,128)(2,1)} %bitcast.24, ...), custom_call_target="tpu_custom_call" | custom-call | tf_op jit(solution)/shard_map/window_grads/pallas_call | solution.py:734
  243.9 0.0 copy-start.1
  243.9 4.0 %copy.26 = bf16[1,256,6144]{2,1,0:T(8,128)(2,1)} copy(bf16[1,256,6144]{2,1,0:T(8,128)(2,1)} %bitcast.23) | data formatting | bytes 6291456
  247.9 0.0 copy-done.1
  247.9 0.0 copy-start.2
  247.9 1.7 copy.27
  249.6 1.1 copy-done.2
  250.6 0.0 copy-start
  250.6 1.3 copy.28
  252.0 1.5 copy-done
  253.4 1.8 copy.29
  (10 shorter events, 0.1 us)
Async XLA Ops:
  243.9 4.0 %copy-start.1 = (bf16[256,6144]{1,0:T(8,128)(2,1)S(1)}, bf16[256,6144]{1,0:T(8,128)(2,1)}, u32[]{:S(2)}) copy-start(bf16[256,6144]{1,0:T(8,128)(2,1)} %get-tuple-element.13) | copy-start | bytes 9437188
  247.9 2.7 %copy-start.2 = (bf16[256,4096]{1,0:T(8,128)(2,1)S(1)}, bf16[256,4096]{1,0:T(8,128)(2,1)}, u32[]{:S(2)}) copy-start(bf16[256,4096]{1,0:T(8,128)(2,1)} %get-tuple-element.14) | copy-start | bytes 6291460
  250.6 2.8 %copy-start = (f32[2,448,1024]{2,1,0:T(8,128)S(1)}, f32[2,448,1024]{2,1,0:T(8,128)}, u32[]{:S(2)}) copy-start(f32[2,448,1024]{2,1,0:T(8,128)} %get-tuple-element.15) | copy-start | bytes 11010052

commit v4 on v3

--- a/solution.py
+++ b/solution.py
@@ -18,6 +18,7 @@
 M_Q, M_G, M_K, M_V, M_DQ, M_MS, M_W, M_DK, M_DV, M_DOT = range(10)
 M_Q_VIA, M_G_VIA, M_DQ_VIA, M_Q_ON, M_G_ON, M_DQ_ON = range(10, 16)
 KINDS = 16
+LIMIT_MIB = 48
 
 E_ACTS, E_ROWS, E_HIGH, E_SPREAD, E_LEVEL, E_AROUND, E_OTHER = range(7)
 
@@ -71,16 +72,16 @@
 
 def attention_kernel(
     pairs,
-    q,
-    k,
-    v,
-    g,
-    rest,
-    dot,
-    acts,
-    high,
-    pieces,
-    lanes,
+    q_in,
+    k_in,
+    v_in,
+    g_in,
+    rest_rows,
+    dot_rows,
+    acts_in,
+    grads_in,
+    counts,
+    lists,
     dq,
     dk,
     dv,
@@ -110,15 +111,33 @@
     g2,
     left,
     right,
-    made,
+    rest,
+    dot,
+    high,
+    pieces,
+    lanes,
+    q,
+    k,
+    v,
+    g,
+    acts,
+    grads,
+    in_sem,
     send,
     recv,
     esend,
     erecv,
     own_sem,
-    out_sem,
 ):
     rows = q.shape[0]
+    loads = [
+        pltpu.make_async_copy(source, held, in_sem.at[at])
+        for at, (source, held) in enumerate(
+            ((k_in, k), (v_in, v), (q_in, q), (g_in, g), (acts_in, acts), (grads_in, grads))
+        )
+    ]
+    for load in loads:
+        load.start()
     me = lax.axis_index("ctx")
     total = lax.axis_size("ctx")
     core = lax.rem(me, 2)
@@ -161,18 +180,18 @@
 
     def message(kind, pair):
         src, dst, target = {
-            M_Q: lambda: (q.at[:, qk_cols(pair)], qn.at[:, qk_cols(pair)], behind_chip),
-            M_G: lambda: (g.at[:, v_cols(pair)], gn.at[:, v_cols(pair)], behind_chip),
-            M_K: lambda: (k.at[:, qk_cols(pair)], ko.at[:, qk_cols(pair)], other),
-            M_V: lambda: (v.at[:, v_cols(pair)], vo.at[:, v_cols(pair)], other),
+            M_Q: lambda: (q_in.at[:, qk_cols(pair)], qn.at[:, qk_cols(pair)], behind_chip),
+            M_G: lambda: (g_in.at[:, v_cols(pair)], gn.at[:, v_cols(pair)], behind_chip),
+            M_K: lambda: (k_in.at[:, qk_cols(pair)], ko.at[:, qk_cols(pair)], other),
+            M_V: lambda: (v_in.at[:, v_cols(pair)], vo.at[:, v_cols(pair)], other),
             M_DQ: lambda: (dqs.at[:, qk_cols(pair)], dq.at[:, qk_cols(pair)], ahead_chip),
             M_MS: lambda: (mss.at[pair], msr.at[pair], ahead_chip),
             M_W: lambda: (ws.at[pair], wr.at[pair], behind_chip),
             M_DK: lambda: (dks.at[:, qk_cols(pair)], dk.at[:, qk_cols(pair)], other),
             M_DV: lambda: (dvs.at[:, v_cols(pair)], dv.at[:, v_cols(pair)], other),
             M_DOT: lambda: (dot, dotn, behind_chip),
-            M_Q_VIA: lambda: (q.at[:, qk_cols(pair)], q_via.at[:, qk_cols(pair)], level),
-            M_G_VIA: lambda: (g.at[:, v_cols(pair)], g_via.at[:, v_cols(pair)], level),
+            M_Q_VIA: lambda: (q_in.at[:, qk_cols(pair)], q_via.at[:, qk_cols(pair)], level),
+            M_G_VIA: lambda: (g_in.at[:, v_cols(pair)], g_via.at[:, v_cols(pair)], level),
             M_DQ_VIA: lambda: (dqs.at[:, qk_cols(pair)], dq_via.at[:, qk_cols(pair)], level),
             M_Q_ON: lambda: (
                 q_via.at[:, qk_cols(pair)],
@@ -339,22 +358,11 @@
             for each in expert_messages(kind):
                 each.wait_send()
 
-    width = made.shape[2]
-    parts = right.shape[2] // width
-
-    def made_copy(index):
-        slot = lax.rem(index, 2)
-        cols = pl.ds(pl.multiple_of(lax.rem(index, parts) * width, 128), width)
-        return pltpu.make_async_copy(
-            made.at[slot], expert.at[lax.div(index, parts), :, cols], out_sem.at[slot]
-        )
+    width = min(expert.shape[2], 256)
+    parts = expert.shape[2] // width
 
     def expert_step(index):
-        @pl.when(index >= 2)
-        def _():
-            made_copy(index - 2).wait()
-
-        mask = lanes[lax.div(index, parts)]
+        mask = lanes[lax.div(index, parts)][0:1].astype(left.dtype)
         cols = pl.ds(pl.multiple_of(lax.rem(index, parts) * width, 128), width)
         result = None
         for low, count in ((0, slots), (slots + 1, slots - 1)):
@@ -363,8 +371,7 @@
             b = right[low : low + count, :, cols].reshape(count * half_rows, width)
             product = plain(a, b)
             result = product if result is None else result + product
-        made[lax.rem(index, 2)] = result
-        made_copy(index).start()
+        expert[lax.div(index, parts), :, cols] = result
 
     barrier = pltpu.get_barrier_semaphore()
     partners = [in_group(partner) for partner in (behind_chip, ahead_chip, other, level)]
@@ -415,11 +422,35 @@
             message(M_DQ_VIA, pair).wait_recv()
             message(M_DQ_ON, pair).start()
 
+    send_chunk(0)
+    for pair in range(pairs):
+        rest[pair] = rest_rows[2 * pair : 2 * pair + 2]
+        dot[pair] = dot_rows[2 * pair : 2 * pair + 2]
+
     @pl.when(has_behind)
     def _():
         message(M_DOT, 0).start()
 
-    send_chunk(0)
+    cap = acts.shape[2]
+    full = [jnp.where(counts[group, slot] == cap, 1.0, 0.0) for slot in range(slots)]
+    row_ids = lax.broadcasted_iota(jnp.int32, (1, half_rows), 1)
+
+    def mark(expert_id, index, value):
+        lanes[expert_id, 0:1, index * half_rows : (index + 1) * half_rows] = value
+
+    for k_ in range(own_slots):
+        for slot in range(own_slots):
+            live = row_ids < counts[group, slot]
+            mark(k_, slot, jnp.where(live, 1.0, 0.0) if slot == k_ else jnp.zeros(row_ids.shape))
+        mark(k_, slots, jnp.zeros(row_ids.shape))
+        mark(k_, slots + 1, jnp.zeros(row_ids.shape) + full[k_])
+        for r in range(replicas):
+            source = lax.rem(group + groups - 1 - r, groups)
+            held = counts[source, own_slots + r]
+            wanted = jnp.where(lists[source, r] == k_, 1.0, 0.0)
+            mark(k_, own_slots + r, jnp.where(row_ids < held, wanted, 0.0))
+            whole = jnp.where(held == cap, wanted, 0.0)
+            mark(k_, slots + 2 + r, jnp.zeros(row_ids.shape) + whole)
 
     lane = lax.broadcasted_iota(jnp.int32, (1, 128), 1)
     low_lanes = jnp.where(lane < 64, 1.0, 0.0).astype(jnp.bfloat16)
@@ -452,6 +483,11 @@
         @pl.when((pair == 0) & has_ahead)
         def _():
             message(M_DOT, 0).wait_recv()
+
+        @pl.when(pair == 0)
+        def _():
+            for load in loads[:4]:
+                load.wait()
 
         for extra, early in ((2 * pair + 1, True), (2 * pair + 2, True), (pair + 3, False)):
             pl.when((extra < pairs) & ((pair < 2) == early))(functools.partial(send_chunk, extra))
@@ -645,6 +681,17 @@
         return carry
 
     def first_stage():
+        for load in loads[4:]:
+            load.wait()
+        full_high, full_piece = 0.0, 0.0
+        for slot in range(slots):
+            full_high = full_high + full[slot] * acts[slot, :, half_rows:].astype(jnp.float32)
+            full_piece = full_piece + full[slot] * grads[slot].astype(jnp.float32)
+        high[...] = full_high.astype(high.dtype)
+        is_upper = jnp.where(upper == 1, 1.0, 0.0)
+        for slot in range(slots):
+            mixed = is_upper * full_piece + (1.0 - is_upper) * grads[slot].astype(jnp.float32)
+            pieces[slot] = mixed.astype(pieces.dtype)
         for each in own_copies():
             each.start()
         begin(E_ROWS, E_HIGH)
@@ -685,8 +732,6 @@
         return carry
 
     lax.fori_loop(0, max(pairs + 3, product_at + products), step_with_experts, 0)
-    for index in range(products - 2, products):
-        made_copy(index).wait()
     left_behind(E_ACTS, E_ROWS, E_HIGH, E_SPREAD, E_LEVEL, E_AROUND, E_OTHER)
 
     @pl.when(has_behind)
@@ -714,16 +759,15 @@
     lax.fori_loop(0, pairs, drain, 0)
 
 
-def gradients(queries, key_states, value_states, out_grad, lse_rest, out_dot, acts, high, pieces, lanes):
+def gradients(queries, key_states, value_states, out_grad, lse_rest, out_dot, acts, grads, counts, lists):
     rows, qk = queries.shape
     vv = value_states.shape[1]
     pairs = qk // PAIR_QK
     slots, features, cap = acts.shape
-    hidden = pieces.shape[2]
-    experts = lanes.shape[0]
+    hidden = grads.shape[2]
+    experts = slots - lists.shape[1]
     groups = lax.axis_size("grp")
     columns = lax.axis_size("ctx") // 4
-    width = min(hidden, 256)
     _, sems = first_sems(groups - 1, groups // 2, columns)
     half = jnp.bfloat16
     vmem = pl.BlockSpec(memory_space=pltpu.VMEM)
@@ -734,16 +778,16 @@
     return pl.pallas_call(
         functools.partial(attention_kernel, pairs),
         out_shape=[
-            jax.ShapeDtypeStruct((rows, qk), half),
-            jax.ShapeDtypeStruct((rows, qk), half),
-            jax.ShapeDtypeStruct((rows, vv), half),
-            jax.ShapeDtypeStruct((experts, features, hidden), jnp.float32),
+            pltpu.VMEM((rows, qk), half),
+            pltpu.VMEM((rows, qk), half),
+            pltpu.VMEM((rows, vv), half),
+            pltpu.VMEM((experts, features, hidden), jnp.float32),
             jax.ShapeDtypeStruct((rows, qk), half),
             jax.ShapeDtypeStruct((rows, vv), half),
             jax.ShapeDtypeStruct((rows, qk), half),
         ],
-        in_specs=[vmem] * 6 + [anywhere] * 3 + [vmem],
-        out_specs=[vmem] * 3 + [anywhere] * 4,
+        in_specs=[anywhere] * 4 + [vmem] * 2 + [anywhere] * 2 + [pl.BlockSpec(memory_space=pltpu.SMEM)] * 2,
+        out_specs=[vmem] * 4 + [anywhere] * 3,
         scratch_shapes=[
             wide,
             narrow,
@@ -767,16 +811,26 @@
             pltpu.VMEM((rows, PAIR_V), half),
             pltpu.VMEM((features, slots * cap), half),
             pltpu.VMEM((2 * slots, cap // 2, hidden), half),
-            pltpu.VMEM((2, features, width), jnp.float32),
+            pltpu.VMEM((pairs, 2, rows), jnp.float32),
+            pltpu.VMEM((pairs, 2, rows), jnp.float32),
+            pltpu.VMEM((features, cap // 2), half),
+            pltpu.VMEM(grads.shape, half),
+            pltpu.VMEM((experts, 8, slots * cap), jnp.float32),
+            wide,
+            wide,
+            narrow,
+            narrow,
+            pltpu.VMEM(acts.shape, half),
+            pltpu.VMEM(grads.shape, half),
+            pltpu.SemaphoreType.DMA((6,)),
             pltpu.SemaphoreType.DMA((KINDS, pairs)),
             pltpu.SemaphoreType.DMA((KINDS, pairs)),
             pltpu.SemaphoreType.DMA((sems,)),
             pltpu.SemaphoreType.DMA((sems,)),
             pltpu.SemaphoreType.DMA((2 * experts + 1,)),
-            pltpu.SemaphoreType.DMA((2,)),
         ],
         compiler_params=pltpu.CompilerParams(
-            collective_id=0, has_side_effects=True, vmem_limit_bytes=60 * 2**20
+            collective_id=0, has_side_effects=True, vmem_limit_bytes=LIMIT_MIB * 2**20
         ),
         name="window_grads",
     )(
@@ -784,61 +838,16 @@
         key_states,
         value_states,
         out_grad,
-        lse_rest.reshape(pairs, 2, rows),
-        out_dot.reshape(pairs, 2, rows),
+        lse_rest,
+        out_dot,
         acts,
-        high,
-        pieces,
-        lanes,
+        grads,
+        counts,
+        lists,
     )[:4]
 
 
-def expert_inputs(acts, grads, counts, replica_list):
-    group = lax.axis_index("grp")
-    groups = lax.axis_size("grp")
-    slots, _, cap = acts.shape
-    replicas = replica_list.shape[1]
-    own = slots - replicas
-    half_rows = cap // 2
-    full = jnp.argmax(counts[group])
-    high = lax.dynamic_slice(acts, (full, 0, half_rows), (1, acts.shape[1], half_rows))[0]
-    full_piece = lax.dynamic_slice_in_dim(grads, full, 1, 0)
-    upper = lax.axis_index("ctx") >= lax.axis_size("ctx") // 2
-    pieces = jnp.where(upper, jnp.broadcast_to(full_piece, grads.shape), grads)
-    block = lax.iota(jnp.int32, slots)
-    behind = jnp.maximum(block - own + 1, 0)
-    source = (group - behind) % groups
-    slot_id = lax.iota(jnp.int32, slots)
-    mine = (source[:, None] == lax.iota(jnp.int32, groups)[None, :]).astype(jnp.int32)
-    my_counts = jnp.sum(mine[:, :, None] * counts[None], 1)
-    my_lists = jnp.sum(mine[:, :, None] * replica_list[None], 1)
-    live = jnp.sum(jnp.where(block[:, None] == slot_id[None, :], my_counts, 0), 1)
-    listed = jnp.sum(
-        jnp.where((block[:, None] - own) == lax.iota(jnp.int32, replicas)[None, :], my_lists, 0), 1
-    )
-    expert = jnp.where(block < own, block, listed)
-    back = jnp.maximum(block - 1, 0)
-    src = (group - back) % groups
-    theirs = (src[:, None] == lax.iota(jnp.int32, groups)[None, :]).astype(jnp.int32)
-    their_counts = jnp.sum(theirs[:, :, None] * counts[None], 1)
-    their_full = jnp.argmax(their_counts, 1)
-    meant = jnp.where(back == 0, their_full < own, their_full == own + back - 1)
-    their_lists = jnp.sum(theirs[:, :, None] * replica_list[None], 1)
-    their_expert = jnp.sum(
-        jnp.where((their_full[:, None] - own) == lax.iota(jnp.int32, replicas)[None, :], their_lists, 0), 1
-    )
-    high_expert = jnp.where(back == 0, their_full, their_expert)
-    high_live = jnp.where(meant & (block >= 1), half_rows, 0)
-    all_live = jnp.concatenate([jnp.minimum(live, half_rows), high_live])
-    all_expert = jnp.concatenate([expert, high_expert])
-    wanted = all_expert[None] == lax.iota(jnp.int32, own)[:, None]
-    keep = lax.iota(jnp.int32, half_rows)[None, None] < jnp.where(wanted, all_live[None], 0)[:, :, None]
-    lanes = keep.astype(jnp.bfloat16).reshape(own, 1, 2 * slots * half_rows)
-    return high, pieces, lanes
-
-
 def local(queries, key_states, value_states, out_grad, lse_rest, out_dot, moe_acts, moe_grads, counts, replica_list):
-    high, pieces, lanes = expert_inputs(moe_acts[0], moe_grads[0], counts, replica_list)
     found = gradients(
         queries[0],
         key_states[0],
@@ -847,9 +856,9 @@
         lse_rest[0],
         out_dot[0],
         moe_acts[0],
-        high,
-        pieces,
-        lanes,
+        moe_grads[0],
+        counts,
+        replica_list,
     )
     return tuple(each[None] for each in found)
 

time: 256 us -> 232 us (0.906)
  local copies, waits for them, and re-layouts: 17.4 us -> 6.48 us
  Pallas kernels: 230 us -> 224 us
  other arithmetic: 5.48 us -> 0 us
    pallas_call x1, Pallas kernels: 230 us -> 224 us  [gradients(): pl.pallas_call(functools.partial(attention_kernel, pairs), out_shape=[plt...]
    unnamed x11 -> x4, local copies, waits for them, and re-layouts: 12.2 us -> 6.48 us
    another operation x2 -> x0, local copies, waits for them, and re-layouts: 2.78 us -> none  [the longest x1 1.39 us: gradients(): lse_rest.reshape(pairs, 2, rows)]
where the time goes in v4:
time: 232 us; the launch traced here: 231 us
  Pallas kernels  224 us (97%)
  local copies, waits for them, and re-layouts  6.48 us (3%)
    pallas_call x1, Pallas kernels, gradients(): pl.pallas_call(functools.partial(attention_kernel, pairs), out_shape=[plt...  224 us
    unnamed x4, local copies, waits for them, and re-layouts  6.48 us

profile of v4, /device:TPU:3, one launch (start us, length us, event | category | flops | bytes accessed | tf_op | source)
XLA Modules:
  0.0 231.1 jit_solution(12493338089889035539)
XLA Ops:
  0.6 224.0 %window_grads.1 = (bf16[256,6144]{1,0:T(8,128)(2,1)S(1)}, bf16[256,6144]{1,0:T(8,128)(2,1)S(1)}, bf16[256,4096]{1,0:T(8,128)(2,1)S(1)}, f32[2,448,1024]{2,1,0:T(...) custom-call(bf16[256,6144]{1,0:T(8,128)(2,1)} %bitcast.16, ...), custom_call_target="tpu_custom_call" | custom-call | tf_op jit(solution)/shard_map/window_grads/pallas_call | solution.py:778
  224.7 1.7 copy.18
  226.3 1.7 copy.19
  228.0 1.3 copy.20
  229.3 1.8 copy.21

commit v5 on v4

--- a/solution.py
+++ b/solution.py
@@ -23,13 +23,13 @@
 E_ACTS, E_ROWS, E_HIGH, E_SPREAD, E_LEVEL, E_AROUND, E_OTHER = range(7)
 
 
-def first_sems(replicas, owners, columns):
+def first_sems(slots, replicas, owners, columns):
     sizes = {
         E_ACTS: replicas,
         E_ROWS: replicas,
         E_HIGH: 1,
         E_SPREAD: 2 * (owners - 1),
-        E_LEVEL: 1,
+        E_LEVEL: slots,
         E_AROUND: 2 * (columns - 1),
         E_OTHER: 2 * columns,
     }
@@ -230,11 +230,17 @@
     owners = groups // 2
     upper = (me >= total // 2).astype(jnp.int32)
     twin = group + 1 - 2 * lax.rem(group, 2)
-    starts, _ = first_sems(replicas, owners, columns)
+    starts, _ = first_sems(slots, replicas, owners, columns)
 
     def unit(device):
         return right.at[
             pl.ds(slots * (device >= total // 2).astype(jnp.int32), slots),
+            pl.ds(pl.multiple_of(lax.rem(device, total // 2) * piece, piece), piece),
+        ]
+
+    def piece_at(device, index):
+        return right.at[
+            slots * (device >= total // 2).astype(jnp.int32) + index,
             pl.ds(pl.multiple_of(lax.rem(device, total // 2) * piece, piece), piece),
         ]
 
@@ -276,11 +282,8 @@
                     kind,
                     r,
                     pieces.at[own_slots + r],
-                    right.at[
-                        slots * upper + own_slots + r,
-                        pl.ds(pl.multiple_of(lax.rem(me, total // 2) * piece, piece), piece),
-                    ],
-                    owner(lax.rem(group + r + 1, groups)),
+                    piece_at(me, own_slots + r),
+                    {"ctx": me if r % 2 else level, "grp": lax.rem(group + r + 1, groups)},
                 )
                 for r in range(replicas)
             ]
@@ -306,7 +309,12 @@
                 )
             return found
         if kind == E_LEVEL:
-            return [expert_message(kind, 0, unit(me), unit(me), in_group(level))]
+            found = []
+            for index in range(slots):
+                away = index >= own_slots and (index - own_slots) % 2 == 0
+                held = piece_at(level if away else me, index)
+                found.append(expert_message(kind, index, held, held, in_group(level)))
+            return found
         if kind == E_AROUND:
             return [
                 expert_message(
@@ -377,6 +385,7 @@
     partners = [in_group(partner) for partner in (behind_chip, ahead_chip, other, level)]
     partners += [in_group(lax.rem(me + 4 * m, total)) for m in range(1, columns)]
     partners += [owner(lax.rem(group + m, groups)) for m in range(1, groups)]
+    partners += [{"ctx": level, "grp": lax.rem(group + m, groups)} for m in range(1, groups, 2)]
     for partner in partners:
         pl.semaphore_signal(barrier, inc=1, device_id=partner, device_id_type=MESH)
     pl.semaphore_wait(barrier, len(partners))
@@ -472,75 +481,84 @@
         return ref[:, pl.ds(pl.multiple_of(pair * PAIR_V + head * V_DIM, 128), V_DIM)]
 
     def first_phase(pair):
-        message(M_K, pair).wait_recv()
-        message(M_V, pair).wait_recv()
-
-        @pl.when(has_ahead)
-        def _():
-            message(M_Q, pair).wait_recv()
-            message(M_G, pair).wait_recv()
-
-        @pl.when((pair == 0) & has_ahead)
-        def _():
-            message(M_DOT, 0).wait_recv()
-
         @pl.when(pair == 0)
         def _():
             for load in loads[:4]:
                 load.wait()
 
-        for extra, early in ((2 * pair + 1, True), (2 * pair + 2, True), (pair + 3, False)):
-            pl.when((extra < pairs) & ((pair < 2) == early))(functools.partial(send_chunk, extra))
-
-        pick_second(pair)
         slot = lax.rem(pair, 3)
         start = pl.multiple_of(pair * PAIR_QK, 128)
         k_own = heads_of(k, start, low_lanes, high_lanes)
-        k_oth = heads_of(ko, start, low_lanes, high_lanes)
         q_own = heads_of(q, start, low_lanes, high_lanes)
-        q_new = heads_of(qn, start, low_lanes, high_lanes)
-        q_sec = heads_of(q2, 0, low_lanes, high_lanes)
         key_pos = lax.broadcasted_iota(jnp.int32, (rows, rows), 0)
         query_pos = lax.broadcasted_iota(jnp.int32, (rows, rows), 1)
         allowed = key_pos <= query_pos
+        dot_own = dot[pair]
+
+        def keep(head, task, prob, grad):
+            pring[slot, head * 3 + task] = prob.astype(jnp.bfloat16)
+            dring[slot, head * 3 + task] = grad.astype(jnp.bfloat16)
+
+        tops_own, sums_own = [], []
+        for head in range(2):
+            s3 = rows_by_rows(k_own[head], q_own[head]) * SCALE
+            s3 = jnp.where(allowed, s3, -1e30)
+            m3 = jnp.max(s3, 0, keepdims=True)
+            p3 = jnp.exp(s3 - m3)
+            g3 = rows_by_rows(v_head(v, pair, head), v_head(g, pair, head))
+            keep(head, 2, p3, p3 * (g3 - dot_own[head : head + 1]))
+            tops_own.append(m3)
+            sums_own.append(jnp.sum(p3, 0, keepdims=True))
+
+        message(M_K, pair).wait_recv()
+        message(M_V, pair).wait_recv()
+
+        @pl.when(has_ahead)
+        def _():
+            message(M_Q, pair).wait_recv()
+            message(M_G, pair).wait_recv()
+
+        @pl.when((pair == 0) & has_ahead)
+        def _():
+            message(M_DOT, 0).wait_recv()
+
+        pl.when(pair == 0)(lambda: send_chunk(1))
+        pl.when(pair + 2 < pairs)(lambda: send_chunk(pair + 2))
+
+        pick_second(pair)
+        k_oth = heads_of(ko, start, low_lanes, high_lanes)
+        q_new = heads_of(qn, start, low_lanes, high_lanes)
+        q_sec = heads_of(q2, 0, low_lanes, high_lanes)
         dot_new = dotn[pair]
-        dot_own = dot[pair]
         dot_sec = c0 * dot_new + c1 * dot_own
-        tops, sums, tops_own, sums_own, dq_heads = [], [], [], [], []
+        lses, tops_sec, sums_sec, dq_heads = [], [], [], []
         for head in range(2):
             s1 = rows_by_rows(k_own[head], q_new[head]) * SCALE
             s2 = rows_by_rows(k_oth[head], q_sec[head]) * SCALE
-            s3 = rows_by_rows(k_own[head], q_own[head]) * SCALE
-            s3 = jnp.where(allowed, s3, -1e30)
             m1 = jnp.max(s1, 0, keepdims=True)
             m2 = jnp.max(s2, 0, keepdims=True)
-            m3 = jnp.max(s3, 0, keepdims=True)
             top_new = jnp.maximum(m1, jnp.where(core_zero, m2, LOW))
-            top_own = jnp.maximum(m3, jnp.where(core_zero, LOW, m2))
-            top_sec = jnp.where(core_zero, top_new, top_own)
+            top_sec = jnp.where(core_zero, top_new, m2)
             p1 = jnp.exp(s1 - top_new)
             p2 = jnp.exp(s2 - top_sec)
-            p3 = jnp.exp(s3 - top_own)
             z1 = jnp.sum(p1, 0, keepdims=True)
             z2 = jnp.sum(p2, 0, keepdims=True)
-            z3 = jnp.sum(p3, 0, keepdims=True)
-            tops.append(top_new)
-            sums.append(z1 + c0 * z2)
-            tops_own.append(top_own)
-            sums_own.append(z3 + c1 * z2)
+            sum_new = z1 + c0 * z2
+            lses.append(top_new + jnp.log(sum_new))
+            inverse = 1.0 / sum_new
+            p1 = p1 * inverse
+            p2 = p2 * jnp.where(core_zero, inverse, 1.0)
+            tops_sec.append(jnp.where(core_zero, LOW, m2))
+            sums_sec.append(z2)
             g1 = rows_by_rows(v_head(v, pair, head), v_head(gn, pair, head))
             g2_ = rows_by_rows(v_head(vo, pair, head), g2[:, head * V_DIM : (head + 1) * V_DIM])
-            g3 = rows_by_rows(v_head(v, pair, head), v_head(g, pair, head))
             d1 = (p1 * (g1 - dot_new[head : head + 1])).astype(jnp.bfloat16)
             d2 = (p2 * (g2_ - dot_sec[head : head + 1])).astype(jnp.bfloat16)
-            d3 = (p3 * (g3 - dot_own[head : head + 1])).astype(jnp.bfloat16)
-            for task, (p_, d_) in enumerate(((p1, d1), (p2, d2), (p3, d3))):
-                pring[slot, head * 3 + task] = p_.astype(jnp.bfloat16)
-                dring[slot, head * 3 + task] = d_
+            keep(head, 0, p1, d1)
+            keep(head, 1, p2, d2)
             dq_heads.append(columns_by_rows(d1, k_own[head]) + c0 * columns_by_rows(d2, k_oth[head]))
-        zero = jnp.zeros((4, rows), jnp.float32)
-        mss[pair] = jnp.concatenate(tops + sums + [zero], 0)
-        own_ms[pair] = jnp.concatenate(tops_own + sums_own + [zero], 0)
+        mss[pair] = jnp.concatenate(lses, 0)
+        own_ms[pair] = jnp.concatenate(tops_own + sums_own + tops_sec + sums_sec, 0)
         store_pair(dqs, start, *dq_heads)
         via = sends_dq_via(pair)
 
@@ -556,19 +574,7 @@
         def _():
             message(M_DQ_VIA, pair).start()
 
-        @pl.when(pair == 1)
-        def _():
-            pass_q_on(1)
-            pass_q_on(2)
-
-        @pl.when(pair == 2)
-        def _():
-            pass_q_on(3)
-            pass_q_on(4)
-
-        @pl.when(pair >= 3)
-        def _():
-            pass_q_on(pair + 2)
+        pl.when(pair >= 1)(lambda: pass_q_on(pair + 1))
 
     def second_phase(pair):
         pass_dq_on(pair)
@@ -580,79 +586,87 @@
         theirs = msr[pair]
         ours = own_ms[pair]
         away = rest[pair]
-        top_far = jnp.where(has_behind, theirs[0:2], LOW)
-        top = jnp.maximum(jnp.maximum(ours[0:2], away), top_far)
+        top_far = jnp.where(has_behind, theirs, LOW)
+        top = jnp.maximum(jnp.maximum(ours[0:2], ours[4:6]), jnp.maximum(away, top_far))
         whole = (
             ours[2:4] * jnp.exp(ours[0:2] - top)
+            + ours[6:8] * jnp.exp(ours[4:6] - top)
             + jnp.exp(away - top)
-            + theirs[2:4] * jnp.exp(top_far - top)
+            + jnp.exp(top_far - top)
         )
         total_lse = top + jnp.log(whole)
-        zero = jnp.zeros((6, rows), jnp.float32)
-        ws[pair] = jnp.concatenate([jnp.exp(top_far - total_lse), zero], 0)
-        fo[pair] = jnp.concatenate([jnp.exp(ours[0:2] - total_lse), zero], 0)
+        ws[pair] = jnp.exp(top_far - total_lse)
+        zero = jnp.zeros((4, rows), jnp.float32)
+        fo[pair] = jnp.concatenate(
+            [jnp.exp(ours[0:2] - total_lse), jnp.exp(ours[4:6] - total_lse), zero], 0
+        )
 
         @pl.when(has_behind)
         def _():
             message(M_W, pair).start()
 
     def third_phase(pair):
-        @pl.when(has_ahead)
-        def _():
-            message(M_W, pair).wait_recv()
-
-        @pl.when(has_behind)
-        def _():
-            message(M_DQ, pair).wait_recv()
-
-        pick_second(pair)
         slot = lax.rem(pair, 3)
         start = pl.multiple_of(pair * PAIR_QK, 128)
         k_own = heads_of(k, start, low_lanes, high_lanes)
+        q_own = heads_of(q, start, low_lanes, high_lanes)
+        own_weight = fo[pair]
+        far_weight = ws[pair]
+        eye = lax.broadcasted_iota(jnp.int32, (rows, rows), 0) == lax.broadcasted_iota(
+            jnp.int32, (rows, rows), 1
+        )
+        acc = lax.rem(pair, 2)
+
+        def scaled(head, task, weight):
+            prob = pring[slot, head * 3 + task].astype(jnp.float32) * weight
+            grad = dring[slot, head * 3 + task].astype(jnp.float32) * (weight * SCALE)
+            return prob.astype(jnp.bfloat16), grad.astype(jnp.bfloat16)
+
+        dq_own, dk_own, columns = [], [], []
+        for head in range(2):
+            prob, grad = scaled(head, 2, own_weight[head : head + 1])
+            accv[acc, :, head * V_DIM : (head + 1) * V_DIM] = plain(prob, v_head(g, pair, head))
+            dk_own.append(plain(grad, q_own[head]))
+            dq_own.append(columns_by_rows(grad, k_own[head]))
+            columns.append(
+                jnp.sum(jnp.where(eye, far_weight[head : head + 1] * SCALE, 0.0), 1, keepdims=True)
+            )
+        store_pair(acck.at[acc], 0, *dk_own)
+
+        @pl.when(has_ahead)
+        def _():
+            message(M_W, pair).wait_recv()
+
+        pick_second(pair)
         k_oth = heads_of(ko, start, low_lanes, high_lanes)
-        q_own = heads_of(q, start, low_lanes, high_lanes)
         q_new = heads_of(qn, start, low_lanes, high_lanes)
         q_sec = heads_of(q2, 0, low_lanes, high_lanes)
         new_weight = wr[pair]
-        own_weight = fo[pair]
-        far_weight = ws[pair]
-        sec_weight = c0 * new_weight + c1 * own_weight
-        eye = lax.broadcasted_iota(jnp.int32, (rows, rows), 0) == lax.broadcasted_iota(
-            jnp.int32, (rows, rows), 1
-        )
-        dq_heads, dk_heads, dko_heads, columns = [], [], [], []
-        acc = lax.rem(pair, 2)
+        sec_weight = c0 * new_weight + c1 * own_weight[2:4]
+        dq_heads, dk_heads, dko_heads = [], [], []
         for head in range(2):
-            weights = [w[head : head + 1] for w in (new_weight, sec_weight, own_weight)]
-            probs = [
-                (pring[slot, head * 3 + t].astype(jnp.float32) * weights[t]).astype(jnp.bfloat16)
-                for t in range(3)
-            ]
-            grads = [
-                (dring[slot, head * 3 + t].astype(jnp.float32) * (weights[t] * SCALE)).astype(
-                    jnp.bfloat16
-                )
-                for t in range(3)
-            ]
-            accv[acc, :, head * V_DIM : (head + 1) * V_DIM] = plain(
-                probs[0], v_head(gn, pair, head)
-            ) + plain(probs[2], v_head(g, pair, head))
+            prob, grad = scaled(head, 1, sec_weight[head : head + 1])
             dvs[:, pl.ds(pl.multiple_of(pair * PAIR_V + head * V_DIM, 128), V_DIM)] = plain(
-                probs[1], g2[:, head * V_DIM : (head + 1) * V_DIM]
+                prob, g2[:, head * V_DIM : (head + 1) * V_DIM]
             ).astype(jnp.bfloat16)
-            dk_heads.append(plain(grads[0], q_new[head]) + plain(grads[2], q_own[head]))
-            dko_heads.append(plain(grads[1], q_sec[head]))
-            dq_heads.append(
-                columns_by_rows(grads[2], k_own[head])
-                + c1 * columns_by_rows(grads[1], k_oth[head])
-            )
-            columns.append(
-                jnp.sum(jnp.where(eye, far_weight[head : head + 1] * SCALE, 0.0), 1, keepdims=True)
-            )
+            dko_heads.append(plain(grad, q_sec[head]))
+            dq_heads.append(dq_own[head] + c1 * columns_by_rows(grad, k_oth[head]))
         store_pair(dks, start, *dko_heads)
         message(M_DV, pair).start()
         message(M_DK, pair).start()
-        store_pair(acck.at[acc], 0, *dk_heads)
+        for head in range(2):
+            prob, grad = scaled(head, 0, new_weight[head : head + 1])
+            accv[acc, :, head * V_DIM : (head + 1) * V_DIM] += plain(prob, v_head(gn, pair, head))
+            dk_heads.append(plain(grad, q_new[head]))
+        even, odd = dk_heads
+        acck[acc, :, :128] += even[:, :128]
+        acck[acc, :, 128:256] += even[:, 128:] + odd[:, :128]
+        acck[acc, :, 256:] += odd[:, 128:]
+
+        @pl.when(has_behind)
+        def _():
+            message(M_DQ, pair).wait_recv()
+
         first = pl.ds(start, 128)
         middle = pl.ds(pl.multiple_of(start + 128, 128), 128)
         last = pl.ds(pl.multiple_of(start + 256, 128), 128)
@@ -697,41 +711,43 @@
         begin(E_ROWS, E_HIGH)
 
     def second_stage():
-        begin(E_ACTS)
-
-    def third_stage():
         for each in own_copies():
             each.wait()
         arrived(E_ROWS, E_HIGH)
         begin(E_LEVEL, E_SPREAD)
 
+    def third_stage():
+        arrived(E_LEVEL)
+
     def fourth_stage():
-        arrived(E_LEVEL)
-        begin(E_AROUND)
-
-    def fifth_stage():
         arrived(E_AROUND)
         begin(E_OTHER)
 
-    def sixth_stage():
+    def fifth_stage():
         arrived(E_OTHER, E_ACTS, E_SPREAD)
 
-    stages = {1: first_stage, 2: second_stage, 3: third_stage, 5: fourth_stage, 8: fifth_stage, 9: sixth_stage}
+    stages = {0: first_stage, 2: second_stage, 3: third_stage, 10: fourth_stage, 11: fifth_stage}
+    spread_out = [(1 + at, each) for at, each in enumerate(expert_messages(E_ACTS))]
+    spread_out += [(3 + at, each) for at, each in enumerate(expert_messages(E_AROUND))]
     products = own_slots * parts
-    product_at = 10
+    product_at, at_once = 11, 2
 
     def step_with_experts(at, carry):
         step(at, carry)
         for when, stage in stages.items():
             pl.when(at == when)(stage)
 
-        @pl.when((at >= product_at) & (at < product_at + products))
-        def _():
-            expert_step(at - product_at)
+        for when, each in spread_out:
+            pl.when(at == when)(each.start)
+
+        @pl.when((at >= product_at) & (at < product_at + products // at_once))
+        def _():
+            for part in range(at_once):
+                expert_step((at - product_at) * at_once + part)
 
         return carry
 
-    lax.fori_loop(0, max(pairs + 3, product_at + products), step_with_experts, 0)
+    lax.fori_loop(0, max(pairs + 3, product_at + products // at_once), step_with_experts, 0)
     left_behind(E_ACTS, E_ROWS, E_HIGH, E_SPREAD, E_LEVEL, E_AROUND, E_OTHER)
 
     @pl.when(has_behind)
@@ -768,11 +784,12 @@
     experts = slots - lists.shape[1]
     groups = lax.axis_size("grp")
     columns = lax.axis_size("ctx") // 4
-    _, sems = first_sems(groups - 1, groups // 2, columns)
+    _, sems = first_sems(slots, groups - 1, groups // 2, columns)
     half = jnp.bfloat16
     vmem = pl.BlockSpec(memory_space=pltpu.VMEM)
     anywhere = pl.BlockSpec(memory_space=pl.ANY)
     small = pltpu.VMEM((pairs, 8, rows), jnp.float32)
+    two_rows = pltpu.VMEM((pairs, 2, rows), jnp.float32)
     wide = pltpu.VMEM((rows, qk), half)
     narrow = pltpu.VMEM((rows, vv), half)
     return pl.pallas_call(
@@ -797,11 +814,11 @@
             wide,
             wide,
             narrow,
+            two_rows,
+            two_rows,
             small,
-            small,
-            small,
-            small,
-            small,
+            two_rows,
+            two_rows,
             small,
             pltpu.VMEM((3, 6, rows, rows), half),
             pltpu.VMEM((3, 6, rows, rows), half),
@@ -847,6 +864,31 @@
     )[:4]
 
 
+def out_kernel(count, *refs):
+    copies = [
+        pltpu.make_async_copy(refs[at], refs[count + at].at[0], refs[2 * count].at[at])
+        for at in range(count)
+    ]
+    for copy in copies:
+        copy.start()
+    for copy in copies:
+        copy.wait()
+
+
+def written_out(found):
+    anywhere = pl.BlockSpec(memory_space=pl.ANY)
+    count = len(found)
+    return pl.pallas_call(
+        functools.partial(out_kernel, count),
+        out_shape=[jax.ShapeDtypeStruct((1, *each.shape), each.dtype) for each in found],
+        in_specs=[pl.BlockSpec(memory_space=pltpu.VMEM)] * count,
+        out_specs=[anywhere] * count,
+        scratch_shapes=[pltpu.SemaphoreType.DMA((count,))],
+        compiler_params=pltpu.CompilerParams(vmem_limit_bytes=24 * 2**20),
+        name="written_out",
+    )(*found)
+
+
 def local(queries, key_states, value_states, out_grad, lse_rest, out_dot, moe_acts, moe_grads, counts, replica_list):
     found = gradients(
         queries[0],
@@ -860,7 +902,7 @@
         counts,
         replica_list,
     )
-    return tuple(each[None] for each in found)
+    return tuple(written_out(found))
 
 
 def solution(mesh):

time: 232 us -> 219 us (0.944)
  local copies, waits for them, and re-layouts: 6.48 us -> 0 us
  Pallas kernels: 224 us -> 218 us
    pallas_call x1, Pallas kernels: 224 us -> 214 us  [gradients(): pl.pallas_call(functools.partial(attention_kernel, pairs), out_shape=[plt...]
    unnamed x4 -> x0, local copies, waits for them, and re-layouts: 6.48 us -> none
    pallas_call x0 -> x1, Pallas kernels: none -> 4.58 us  [written_out(): pl.pallas_call(functools.partial(out_kernel, count), out_shape=[jax.Shape...]
where the time goes in v5:
time: 219 us
  Pallas kernels  218 us (100%)
    pallas_call x1, Pallas kernels, gradients(): pl.pallas_call(functools.partial(attention_kernel, pairs), out_shape=[plt...  214 us
    pallas_call x1, Pallas kernels, written_out(): pl.pallas_call(functools.partial(out_kernel, count), out_shape=[jax.Shape...  4.58 us

profile of v5, /device:TPU:3, one launch (start us, length us, event | category | flops | bytes accessed | tf_op | source)
XLA Modules:
  0.0 218.8 jit_solution(4546266764882161865)
XLA Ops:
  0.6 213.6 %window_grads.1 = (bf16[256,6144]{1,0:T(8,128)(2,1)S(1)}, bf16[256,6144]{1,0:T(8,128)(2,1)S(1)}, bf16[256,4096]{1,0:T(8,128)(2,1)S(1)}, f32[2,448,1024]{2,1,0:T(...) custom-call(bf16[256,6144]{1,0:T(8,128)(2,1)} %bitcast.8, ...), custom_call_target="tpu_custom_call" | custom-call | tf_op jit(solution)/shard_map/window_grads/pallas_call | solution.py:795
  214.2 4.6 %written_out.1 = (bf16[1,256,6144]{2,1,0:T(8,128)(2,1)}, bf16[1,256,6144]{2,1,0:T(8,128)(2,1)}, bf16[1,256,4096]{2,1,0:T(8,128)(2,1)}, f32[1,2,448,1024]{3,2,1,0:T(8,128)}) custom-call(bf16[256,6144]{1,0:T(8,128)(2,1)S(1)} %get-tuple-element.8.refs_0_, bf16[256,6144]{1,0:T(8,128)(2,1)S(1)} %get-tuple-element.9.refs_1_, ...), custom_call_target="tpu_custom_call" | custom-call | tf_op jit(solution)/shard_map/written_out/pallas_call | solution.py:881

commit v6 on v5

--- a/solution.py
+++ b/solution.py
@@ -19,6 +19,7 @@
 M_Q_VIA, M_G_VIA, M_DQ_VIA, M_Q_ON, M_G_ON, M_DQ_ON = range(10, 16)
 KINDS = 16
 LIMIT_MIB = 48
+DRAIN_LAG = 5
 
 E_ACTS, E_ROWS, E_HIGH, E_SPREAD, E_LEVEL, E_AROUND, E_OTHER = range(7)
 
@@ -510,6 +511,7 @@
             tops_own.append(m3)
             sums_own.append(jnp.sum(p3, 0, keepdims=True))
 
+        pl.when(pair == 0)(lambda: send_chunk(1))
         message(M_K, pair).wait_recv()
         message(M_V, pair).wait_recv()
 
@@ -522,7 +524,6 @@
         def _():
             message(M_DOT, 0).wait_recv()
 
-        pl.when(pair == 0)(lambda: send_chunk(1))
         pl.when(pair + 2 < pairs)(lambda: send_chunk(pair + 2))
 
         pick_second(pair)
@@ -732,28 +733,6 @@
     products = own_slots * parts
     product_at, at_once = 11, 2
 
-    def step_with_experts(at, carry):
-        step(at, carry)
-        for when, stage in stages.items():
-            pl.when(at == when)(stage)
-
-        for when, each in spread_out:
-            pl.when(at == when)(each.start)
-
-        @pl.when((at >= product_at) & (at < product_at + products // at_once))
-        def _():
-            for part in range(at_once):
-                expert_step((at - product_at) * at_once + part)
-
-        return carry
-
-    lax.fori_loop(0, max(pairs + 3, product_at + products // at_once), step_with_experts, 0)
-    left_behind(E_ACTS, E_ROWS, E_HIGH, E_SPREAD, E_LEVEL, E_AROUND, E_OTHER)
-
-    @pl.when(has_behind)
-    def _():
-        message(M_DOT, 0).wait_send()
-
     def drain(pair, carry):
         def settle(condition, *kinds):
             @pl.when(condition)
@@ -772,7 +751,36 @@
         settle(passes_dq_on(pair), M_DQ_ON)
         return carry
 
-    lax.fori_loop(0, pairs, drain, 0)
+    def sixth_stage():
+        left_behind(E_ACTS, E_ROWS, E_HIGH, E_SPREAD, E_LEVEL, E_AROUND, E_OTHER)
+
+    stages[product_at + products // at_once] = sixth_stage
+    steps = max(pairs + 3, product_at + products // at_once + 1)
+    settled = min(max(steps - DRAIN_LAG, 0), pairs)
+
+    def step_with_experts(at, carry):
+        step(at, carry)
+        for when, stage in stages.items():
+            pl.when(at == when)(stage)
+
+        for when, each in spread_out:
+            pl.when(at == when)(each.start)
+
+        @pl.when((at >= product_at) & (at < product_at + products // at_once))
+        def _():
+            for part in range(at_once):
+                expert_step((at - product_at) * at_once + part)
+
+        pl.when((at >= DRAIN_LAG) & (at < settled + DRAIN_LAG))(lambda: drain(at - DRAIN_LAG, None))
+        return carry
+
+    lax.fori_loop(0, steps, step_with_experts, 0)
+
+    @pl.when(has_behind)
+    def _():
+        message(M_DOT, 0).wait_send()
+
+    lax.fori_loop(settled, pairs, drain, 0)
 
 
 def gradients(queries, key_states, value_states, out_grad, lse_rest, out_dot, acts, grads, counts, lists):

time: 219 us -> 216 us (0.986); the launches traced: 219 us -> 213 us
  Pallas kernels: 218 us -> 212 us
    pallas_call x1, Pallas kernels: 214 us -> 207 us  [gradients(): pl.pallas_call(functools.partial(attention_kernel, pairs), out_shape=[plt...]
where the time goes in v6:
time: 216 us; the launch traced here: 213 us
  Pallas kernels  212 us (98%)
    pallas_call x1, Pallas kernels, gradients(): pl.pallas_call(functools.partial(attention_kernel, pairs), out_shape=[plt...  207 us
    pallas_call x1, Pallas kernels, written_out(): pl.pallas_call(functools.partial(out_kernel, count), out_shape=[jax.Shape...  4.58 us

profile of v6, /device:TPU:3, one launch (start us, length us, event | category | flops | bytes accessed | tf_op | source)
XLA Modules:
  0.0 212.6 jit_solution(10514648074427304394)
XLA Ops:
  0.6 207.4 %window_grads.1 = (bf16[256,6144]{1,0:T(8,128)(2,1)S(1)}, bf16[256,6144]{1,0:T(8,128)(2,1)S(1)}, bf16[256,4096]{1,0:T(8,128)(2,1)S(1)}, f32[2,448,1024]{2,1,0:T(...) custom-call(bf16[256,6144]{1,0:T(8,128)(2,1)} %bitcast.8, ...), custom_call_target="tpu_custom_call" | custom-call | tf_op jit(solution)/shard_map/window_grads/pallas_call | solution.py:803
  208.0 4.6 %written_out.1 = (bf16[1,256,6144]{2,1,0:T(8,128)(2,1)}, bf16[1,256,6144]{2,1,0:T(8,128)(2,1)}, bf16[1,256,4096]{2,1,0:T(8,128)(2,1)}, f32[1,2,448,1024]{3,2,1,0:T(8,128)}) custom-call(bf16[256,6144]{1,0:T(8,128)(2,1)S(1)} %get-tuple-element.8.refs_0_, bf16[256,6144]{1,0:T(8,128)(2,1)S(1)} %get-tuple-element.9.refs_1_, ...), custom_call_target="tpu_custom_call" | custom-call | tf_op jit(solution)/shard_map/written_out/pallas_call | solution.py:889

commit v7 on v6

--- a/solution.py
+++ b/solution.py
@@ -391,6 +391,38 @@
         pl.semaphore_signal(barrier, inc=1, device_id=partner, device_id_type=MESH)
     pl.semaphore_wait(barrier, len(partners))
 
+    def send_chunk(pair):
+        via = sends_q_via(pair)
+
+        @pl.when(has_behind & jnp.logical_not(via))
+        def _():
+            message(M_Q, pair).start()
+            message(M_G, pair).start()
+
+        @pl.when(via)
+        def _():
+            message(M_Q_VIA, pair).start()
+            message(M_G_VIA, pair).start()
+
+        message(M_K, pair).start()
+        message(M_V, pair).start()
+
+    def pass_q_on(pair):
+        @pl.when((pair < pairs) & passes_q_on(pair))
+        def _():
+            message(M_Q_VIA, pair).wait_recv()
+            message(M_Q_ON, pair).start()
+            message(M_G_VIA, pair).wait_recv()
+            message(M_G_ON, pair).start()
+
+    def pass_dq_on(pair):
+        @pl.when(passes_dq_on(pair))
+        def _():
+            message(M_DQ_VIA, pair).wait_recv()
+            message(M_DQ_ON, pair).start()
+
+    send_chunk(0)
+
     @pl.when(jnp.logical_not(has_ahead))
     def _():
         qn[...] = jnp.zeros_like(qn)
@@ -403,36 +435,6 @@
         msr[...] = jnp.zeros_like(msr)
         dq[...] = jnp.zeros_like(dq)
 
-    def send_chunk(pair):
-        message(M_K, pair).start()
-        message(M_V, pair).start()
-        via = sends_q_via(pair)
-
-        @pl.when(has_behind & jnp.logical_not(via))
-        def _():
-            message(M_Q, pair).start()
-            message(M_G, pair).start()
-
-        @pl.when(via)
-        def _():
-            message(M_Q_VIA, pair).start()
-            message(M_G_VIA, pair).start()
-
-    def pass_q_on(pair):
-        @pl.when((pair < pairs) & passes_q_on(pair))
-        def _():
-            message(M_Q_VIA, pair).wait_recv()
-            message(M_Q_ON, pair).start()
-            message(M_G_VIA, pair).wait_recv()
-            message(M_G_ON, pair).start()
-
-    def pass_dq_on(pair):
-        @pl.when(passes_dq_on(pair))
-        def _():
-            message(M_DQ_VIA, pair).wait_recv()
-            message(M_DQ_ON, pair).start()
-
-    send_chunk(0)
     for pair in range(pairs):
         rest[pair] = rest_rows[2 * pair : 2 * pair + 2]
         dot[pair] = dot_rows[2 * pair : 2 * pair + 2]

time: 216 us -> 216 us (level)
  no operation moved by 1% of the time
where the time goes in v7:
time: 216 us; the launch traced here: 213 us
  Pallas kernels  212 us (98%)
    pallas_call x1, Pallas kernels, gradients(): pl.pallas_call(functools.partial(attention_kernel, pairs), out_shape=[plt...  207 us
    pallas_call x1, Pallas kernels, written_out(): pl.pallas_call(functools.partial(out_kernel, count), out_shape=[jax.Shape...  4.58 us

profile of v7, /device:TPU:3, one launch (start us, length us, event | category | flops | bytes accessed | tf_op | source)
XLA Modules:
  0.0 212.6 jit_solution(6245037831460311429)
XLA Ops:
  0.6 207.4 %window_grads.1 = (bf16[256,6144]{1,0:T(8,128)(2,1)S(1)}, bf16[256,6144]{1,0:T(8,128)(2,1)S(1)}, bf16[256,4096]{1,0:T(8,128)(2,1)S(1)}, f32[2,448,1024]{2,1,0:T(...) custom-call(bf16[256,6144]{1,0:T(8,128)(2,1)} %bitcast.8, ...), custom_call_target="tpu_custom_call" | custom-call | tf_op jit(solution)/shard_map/window_grads/pallas_call | solution.py:805
  208.0 4.6 %written_out.1 = (bf16[1,256,6144]{2,1,0:T(8,128)(2,1)}, bf16[1,256,6144]{2,1,0:T(8,128)(2,1)}, bf16[1,256,4096]{2,1,0:T(8,128)(2,1)}, f32[1,2,448,1024]{3,2,1,0:T(8,128)}) custom-call(bf16[256,6144]{1,0:T(8,128)(2,1)S(1)} %get-tuple-element.8.refs_0_, bf16[256,6144]{1,0:T(8,128)(2,1)S(1)} %get-tuple-element.9.refs_1_, ...), custom_call_target="tpu_custom_call" | custom-call | tf_op jit(solution)/shard_map/written_out/pallas_call | solution.py:891
